TPU v7x, 512 devices: a whole 4x8x8 slice. The times are simulated.
512 devices in a mesh: gx: 8 (over y_lo, core), gy: 8 (over y_hi, x), gz: 8 (over z).
Axes of the slice: x: 4, y: 8 (y_hi: 2, y_lo: 4; y = y_hi * 4 + y_lo), z: 8, core: 2. Of those that a mesh axis runs over, the one named last changes fastest.
Arguments:
- positions: float32 [512, 3, 72], P(('gx', 'gy', 'gz')), may hold values from 0.6 to 11.4, as said below
- species: int32 [512, 72], P(('gx', 'gy', 'gz')), may hold values from 0 to 3
- site_atom: int32 [512, 72], P(('gx', 'gy', 'gz')), may hold values from 0 to 71, as said below
- edge_center: int32 [512, 1152], P(('gx', 'gy', 'gz')), may hold values from 0 to 71, as said below
- edge_other: int32 [512, 1152], P(('gx', 'gy', 'gz')), may hold values from 0 to 255, as said below
- edge_count: int32 [512], P(('gx', 'gy', 'gz')), may hold values from 240 to 1152, as said below
- w_in: float32 [128, 16], replicated, may hold values from -1.5 to 1.5
- w_two: float32 [64, 128], replicated, may hold values from -0.5 to 0.5
- w_env: float32 [64, 64], replicated, may hold values from -0.75 to 0.75
- w_value: float32 [64, 64], replicated, may hold values from -0.75 to 0.75
- w_latent: float32 [128, 256], replicated, may hold values from -0.375 to 0.375
- w_out: float32 [64, 128], replicated, may hold values from -0.5 to 0.5
- readout: float32 [64], replicated, may hold values from -0.75 to 0.75
Outputs:
- forces: float32 [512, 3, 72], P(('gx', 'gy', 'gz'))
- site_energy: float32 [512, 72], P(('gx', 'gy', 'gz'))
- virial: float32 [3, 3], replicated
Inputs may be any that keep to these rules, and one draw needn't show every extreme that they name: `positions`: the atom at lattice site (i, j, k) has coordinates within 0.4 of (2 i + 1, 2 j + 1, 2 k + 1). `site_atom`: each domain's row is a permutation of its atoms. `edge_center`: each atom is the center of exactly 16 slots of its domain. `edge_other`: the cell of the extended grid one of the 26 nonzero steps away from the center's own cell (its site (i, j, k) sits at cell (i + 1, j + 1, k + 1)); the 16 slots of one center take distinct steps. `edge_count`: edge slots at or after a domain's count are padding.
All inputs are finite; a program needn't handle non-finite values.
Results may differ from a plain program's by a relative error of at most 0.0003.
Values sent between devices are 32-bit elements; how exact they have to be, the bound alone decides.
No kernel may reach another device: no remote copies, remote signals or barrier semaphores. Data moves between devices by JAX's collectives and lax.ppermute only.
A program may use at most 64 MiB of HBM per device.

v0:
```python
import math

import jax
import jax.numpy as jnp
from jax import lax
from jax.sharding import PartitionSpec as P

CELLS = 6
LAYERS = 2
RADIAL = 8
SPECIES = 4


spacing = 2.0
cutoff = 5.0
highest = lax.Precision.HIGHEST


def extended_2(block, sides, width):
    for axis, dim in sides:
        count = lax.axis_size(axis)
        forward = [(i, i + 1) for i in range(count - 1)]
        forward.append((count - 1, 0))
        backward = [(target, source) for source, target in forward]
        low = lax.ppermute(
            lax.slice_in_dim(block, block.shape[dim] - width, None, axis=dim), axis, forward
        )
        high = lax.ppermute(lax.slice_in_dim(block, 0, width, axis=dim), axis, backward)
        block = jnp.concatenate([low, block, high], axis=dim)
    return block


def matmul(left, right):
    return jnp.dot(left, right, precision=highest, preferred_element_type=jnp.float32)


def harmonics(displacement):
    comp_x = displacement[0] / cutoff
    comp_y = displacement[1] / cutoff
    comp_z = displacement[2] / cutoff
    root_three = math.sqrt(3.0)
    return jnp.stack(
        [
            jnp.ones_like(comp_x),
            comp_x,
            comp_y,
            comp_z,
            root_three * comp_x * comp_y,
            root_three * comp_y * comp_z,
            root_three * comp_x * comp_z,
            0.5 * root_three * (comp_x * comp_x - comp_y * comp_y),
            0.5 * (2.0 * comp_z * comp_z - comp_x * comp_x - comp_y * comp_y),
        ],
        axis=0,
    )


def step_table():
    sign_rows = []
    for cell_count in (CELLS, CELLS, LAYERS):
        cell_ids = jnp.arange(cell_count + 2, dtype=jnp.int32)
        upper_side = (cell_ids == cell_count + 1).astype(jnp.float32)
        lower_side = (cell_ids == 0).astype(jnp.float32)
        sign_rows.append(spacing * cell_count * (upper_side - lower_side))
    grid_shape = (CELLS + 2, CELLS + 2, LAYERS + 2)
    return jnp.stack(
        [
            jnp.broadcast_to(sign_rows[0][:, None, None], grid_shape),
            jnp.broadcast_to(sign_rows[1][None, :, None], grid_shape),
            jnp.broadcast_to(sign_rows[2][None, None, :], grid_shape),
        ],
        axis=0,
    ).reshape(3, -1)


def domain_energy(
    local_pos, extended_pos, local_kind, extended_kind, center, partner, live_count, weights
):
    w_in, w_two, w_env, w_value, w_latent, w_out, readout = weights
    atom_count = local_pos.shape[1]
    edge_total = center.shape[0]
    channels = w_env.shape[0]
    displacement = jnp.take(extended_pos, partner, axis=1) - jnp.take(local_pos, center, axis=1)
    scaled_sq = jnp.sum(displacement * displacement, axis=0) / (cutoff * cutoff)
    envelope = (1.0 - scaled_sq) * (1.0 - scaled_sq)
    live_mask = (jnp.arange(edge_total, dtype=jnp.int32) < live_count).astype(jnp.float32)
    orders = jnp.arange(RADIAL, dtype=jnp.int32).astype(jnp.float32)[:, None]
    radial = jnp.cos(math.pi * orders * scaled_sq[None, :])
    species_ids = jnp.arange(SPECIES, dtype=jnp.int32)[:, None]
    center_kind = (jnp.take(local_kind, center)[None, :] == species_ids).astype(jnp.float32)
    partner_kind = (jnp.take(extended_kind, partner)[None, :] == species_ids).astype(jnp.float32)
    inputs = jnp.concatenate([radial, center_kind, partner_kind], axis=0)
    two_body = matmul(w_two, jax.nn.silu(matmul(w_in, inputs)))
    weight_env = matmul(w_env, two_body) * (envelope * live_mask)[None, :]
    values = matmul(w_value, two_body)
    harmonic = harmonics(displacement)
    outer_terms = (harmonic[:, None, :] * weight_env[None, :, :]).reshape(9 * channels, edge_total)
    environment = jnp.zeros((9 * channels, atom_count), jnp.float32).at[:, center].add(outer_terms)
    at_edges = (
        jnp.take(environment, center, axis=1).reshape(9, channels, edge_total)
        * harmonic[:, None, :]
    )
    path_zero = at_edges[0]
    path_one = at_edges[1] + at_edges[2] + at_edges[3]
    path_two = at_edges[4] + at_edges[5] + at_edges[6] + at_edges[7] + at_edges[8]
    latent_in = jnp.concatenate(
        [two_body, path_zero * values, path_one * values, path_two * values], axis=0
    )
    latent = matmul(w_out, jax.nn.silu(matmul(w_latent, latent_in)))
    edge_energy = matmul(readout, latent) * envelope * live_mask
    return jnp.zeros((atom_count,), jnp.float32).at[center].add(edge_energy)


def fetch_ghosts(site_grid):
    arrived = extended_2(site_grid, (("gx", 1), ("gy", 2), ("gz", 3)), 1)
    return arrived


def return_ghosts(grad_grid):
    arrived = extended_2(grad_grid, (("gx", 1), ("gy", 2), ("gz", 3)), 1)
    return arrived


def fold_back(block, axis_dim):
    cell_count = block.shape[axis_dim] - 4
    middle_part = lax.slice_in_dim(block, 2, cell_count + 2, axis=axis_dim)
    lower_rim = lax.slice_in_dim(block, 0, 1, axis=axis_dim)
    upper_rim = lax.slice_in_dim(block, cell_count + 3, cell_count + 4, axis=axis_dim)
    lower_pads = [(0, 0)] * block.ndim
    lower_pads[axis_dim] = (0, cell_count - 1)
    upper_pads = [(0, 0)] * block.ndim
    upper_pads[axis_dim] = (cell_count - 1, 0)
    return middle_part + jnp.pad(lower_rim, lower_pads) + jnp.pad(upper_rim, upper_pads)


def body(
    positions,
    species,
    site_atom,
    edge_center,
    edge_other,
    edge_count,
    w_in,
    w_two,
    w_env,
    w_value,
    w_latent,
    w_out,
    readout,
):
    local_pos = positions[0]
    local_kind = species[0]
    sites_order = site_atom[0]
    atom_count = local_pos.shape[1]
    site_grid = jnp.concatenate(
        [
            jnp.take(local_pos, sites_order, axis=1),
            jnp.take(local_kind, sites_order)[None, :].astype(jnp.float32),
        ],
        axis=0,
    ).reshape(4, CELLS, CELLS, LAYERS)
    extended = fetch_ghosts(site_grid).reshape(4, -1)
    extended_pos = extended[:3] + step_table()
    extended_kind = extended[3].astype(jnp.int32)
    weights = (w_in, w_two, w_env, w_value, w_latent, w_out, readout)
    center = edge_center[0]
    partner = edge_other[0]
    live_count = edge_count[0]

    def energy_of(first, second):
        return domain_energy(
            first, second, local_kind, extended_kind, center, partner, live_count, weights
        )

    site_energy, pullback = jax.vjp(energy_of, local_pos, extended_pos)
    g_local, g_extended = pullback(jnp.ones_like(site_energy))
    virial_part = -(matmul(local_pos, g_local.T) + matmul(extended_pos, g_extended.T))
    grad_grid = g_extended.reshape(3, CELLS + 2, CELLS + 2, LAYERS + 2)
    gathered_grad = return_ghosts(grad_grid)
    site_grad = fold_back(fold_back(fold_back(gathered_grad, 1), 2), 3).reshape(3, atom_count)
    summed = g_local + jnp.zeros_like(g_local).at[:, sites_order].add(site_grad)
    devices = lax.axis_size("gx") * lax.axis_size("gy") * lax.axis_size("gz")
    normalizer = 1.0 / math.sqrt(edge_center.shape[1] * devices)
    virial = lax.psum(virial_part, ("gx", "gy", "gz")) * normalizer
    return ((-summed)[None], site_energy[None], virial)


def solution(mesh):
    placed = (
        P(("gx", "gy", "gz"), None, None),
        P(("gx", "gy", "gz"), None),
        P(("gx", "gy", "gz"), None),
        P(("gx", "gy", "gz"), None),
        P(("gx", "gy", "gz"), None),
        P(("gx", "gy", "gz")),
        P(),
        P(),
        P(),
        P(),
        P(),
        P(),
        P(),
    )
    return jax.shard_map(
        body,
        mesh=mesh,
        in_specs=placed,
        out_specs=(P(("gx", "gy", "gz"), None, None), P(("gx", "gy", "gz"), None), P()),
        check_vma=False,
    )
```

profile of v0, /device:TPU:1, one launch (start us, length us, event | category | flops | bytes accessed | tf_op | source)
XLA Modules:
  0.0 298.5 jit_solution(5778409550646235616)
XLA Ops:
  0.7 0.7 fusion.91
  1.4 0.5 broadcast.480
  1.9 1.3 reduce.19
  3.2 1.6 gather_fusion.1
  4.8 0.7 convert_reduce_fusion
  6.0 0.8 copy.145
  6.8 0.6 gather_fusion
  7.6 4.6 %collective-permute-start = (f32[4,1,6,2]{2,1,3,0:T(1,128)S(1)}, f32[4,1,6,2]{2,1,3,0:T(1,128)S(1)}, u32[]{:S(2)}, u32[]{:S(2)}) collective-permute-start(f32[4,1,6,2]{2,1,3,0:T(1,128)S(1)} %get-tuple-element.51), channel_id=1, source_target_pairs={{0,64},{64,128},{128,192},{192,256},{256,320},{320,384},{384,448},... | collective-permute-start | bytes 584 | tf_op jit(solution)/shard_map/ppermute | solution.py:25
  12.2 6.1 %collective-permute-start.1 = (f32[4,1,6,2]{2,1,3,0:T(1,128)S(1)}, f32[4,1,6,2]{2,1,3,0:T(1,128)S(1)}, u32[]{:S(2)}, u32[]{:S(2)}) collective-permute-start(f32[4,1,6,2]{2,1,3,0:T(1,128)S(1)} %get-tuple-element.52), channel_id=1, source_target_pairs={{64,0},{128,64},{192,128},{256,192},{320,256},{384,320},{448,384},... | collective-permute-start | bytes 584 | tf_op jit(solution)/shard_map/ppermute | solution.py:28
  18.3 0.7 fusion.81
  19.0 0.7 fusion.82
  19.9 1.9 collective-permute-start.2
  21.8 9.4 %collective-permute-start.3 = (f32[4,8,1,2]{2,1,3,0:T(8,128)S(1)}, f32[4,8,1,2]{2,1,3,0:T(8,128)S(1)}, u32[]{:S(2)}, u32[]{:S(2)}) collective-permute-start(f32[4,8,1,2]{2,1,3,0:T(8,128)S(1)} %get-tuple-element.50), channel_id=1, source_target_pairs={{8,0},{16,8},{24,16},{32,24},{40,32},{48,40},{56,48},{0,56},{9,1},... | collective-permute-start | bytes 776 | tf_op jit(solution)/shard_map/ppermute | solution.py:28
  31.3 0.9 collective-permute-done.3
  32.4 1.9 collective-permute-start.4
  34.3 8.0 %collective-permute-start.5 = (f32[4,8,8,1]{2,1,3,0:T(8,128)S(1)}, f32[4,8,8,1]{2,1,3,0:T(8,128)S(1)}, u32[]{:S(2)}, u32[]{:S(2)}) collective-permute-start(f32[4,8,8,1]{2,1,3,0:T(8,128)S(1)} %get-tuple-element.48), channel_id=1, source_target_pairs={{1,0},{2,1},{3,2},{4,3},{5,4},{6,5},{7,6},{0,7},{9,8},{10,9},{11,1... | collective-permute-start | bytes 3080 | tf_op jit(solution)/shard_map/ppermute | solution.py:28
  42.3 7.0 %gather_fusion.4 = s32[1152]{0:T(1024)S(1)} fusion(s32[72]{0:T(128)S(1)} %bitcast.126, s32[2048]{0:T(1024)S(1)} %pad_clamp_fusion), kind=kCustom, calls=%fused_computation.4 | custom fusion | bytes 13824 | tf_op jit(solution)/shard_map/jvp(jit(_take))/gather | solution.py:90
  49.2 2.4 gather_fusion.3
  52.4 7.0 %gather_fusion.7 = f32[1152]{0:T(1024)S(1)} fusion(f32[72]{0:T(128)S(1)} %broadcast_in_dim.140, s32[2048]{0:T(1024)S(1)} %pad_clamp_fusion), kind=kCustom, calls=%fused_computation.7 | custom fusion | bytes 13824 | tf_op jit(solution)/shard_map/transpose(jvp())/gather | solution.py:111
  60.0 7.3 %gather_fusion.5 = s32[1152]{0:T(1024)S(1)} fusion(s32[256]{0:T(256)S(1)} %convert_element_type.83, s32[2048]{0:T(1024)S(1)} %pad_clamp_fusion.1), kind=kCustom, calls=%fused_computation.5 | custom fusion | bytes 13824 | tf_op jit(solution)/shard_map/jvp(jit(_take))/gather | solution.py:91
  67.8 2.4 gather_fusion.2
  70.6 0.6 fusion.80
  71.2 0.6 copy-done.25
  72.0 1.1 convolution_bitcast_fusion.4
  73.2 0.9 fusion.26
  74.1 1.1 convolution_bitcast_fusion.7
  75.2 1.1 broadcast_multiply_fusion.2
  76.4 1.7 broadcast_multiply_fusion
  78.2 2.7 copy.152
  80.9 10.9 %scatter_custom_fusion = f32[576,72]{0,1:T(8,128)S(1)} fusion(s32[1152]{0:T(1024)S(1)} %fusion.81, f32[576,1152]{0,1:T(8,128)S(1)} %copy.152, f32[]{:T(128)} %constant.96.clone.1), kind=kCustom, calls=%fused_computation.17 | custom fusion | flops 663552 | bytes 3115012 | tf_op jit(solution)/shard_map/jvp()/scatter-add | solution.py:98
  91.8 4.7 %gather_fusion.6 = f32[1152,576]{1,0:T(8,128)} fusion(f32[576,72]{0,1:T(8,128)S(1)} %scatter_custom_fusion, s32[2048]{0:T(1024)S(1)} %pad_clamp_fusion), kind=kCustom, calls=%fused_computation.6 | custom fusion | bytes 5313024 | tf_op jit(solution)/shard_map/jvp(jit(_take))/gather | solution.py:100
  96.5 2.6 copy.153
  99.3 0.7 copy-done.7
  100.1 0.9 fusion.108
  101.2 2.0 convolution_bitcast_fusion.2
  103.3 1.6 convolution_bitcast_fusion.9
  104.9 0.7 convolution_bitcast_fusion.3
  105.6 1.3 convolution_bitcast_fusion
  107.0 1.0 copy-done.14
  108.1 0.7 copy-done.6
  108.8 1.6 broadcast_multiply_fusion.1
  110.4 3.5 %copy.154 = f32[576,1152]{0,1:T(8,128)} copy(f32[576,1152]{1,0:T(8,128)} %bitcast.132) | data formatting | bytes 5308416 | tf_op jit(solution)/shard_map/transpose(jvp())/reshape | solution.py:100
  113.9 11.6 %scatter_custom_fusion.1 = f32[576,72]{0,1:T(8,128)S(1)} fusion(s32[1152]{0:T(1024)} %copy-done.34, f32[576,1152]{0,1:T(8,128)} %copy.154, f32[]{:T(128)} %constant.96.clone.1), kind=kCustom, calls=%fused_computation.15 | custom fusion | flops 663552 | bytes 3115520 | tf_op jit(solution)/shard_map/transpose(jvp(jit(_take)))/scatter-add | solution.py:100
  125.5 4.7 %gather_fusion.8 = f32[1152,576]{1,0:T(8,128)} fusion(f32[576,72]{0,1:T(8,128)S(1)} %scatter_custom_fusion.1, s32[2048]{0:T(1024)S(1)} %pad_clamp_fusion), kind=kCustom, calls=%fused_computation.8 | custom fusion | bytes 5313024 | tf_op jit(solution)/shard_map/transpose(jvp())/gather | solution.py:98
  130.2 3.5 %copy.155 = f32[576,1152]{1,0:T(8,128)} copy(f32[576,1152]{0,1:T(8,128)} %bitcast.129) | data formatting | bytes 5308416 | tf_op jit(solution)/shard_map/transpose(jvp())/gather | solution.py:98
  133.8 3.0 %multiply_reduce_fusion.1 = (f32[9,1152]{1,0:T(8,128)S(1)}, f32[64,1152]{1,0:T(8,128)S(1)}, f32[9,1152]{1,0:T(8,128)S(1)}) fusion(f32[9,64,1152]{2,1,0:T(8,128)} %bitcast.131, f32[64,1152]{1,0:T(8,128)S(1)} %copy-done.4, pred[1152]{0:T(1024)(128)(4,1)} %copy-done.29, f32[9,1152]{1,0:T(8,128)S(1)} %stack.5, f32[1,64,1152]{2,1,0:T(8,128)} %copy-done.5, ...), kind=kLoop, calls=%fused_computation.21 | loop fusion | flops 10522368 | bytes 6908544 | tf_op jit(solution)/shard_map/transpose(jvp())/reduce_sum | solution.py:97
  137.3 2.1 fusion.5
  139.5 0.4 fusion.4
  140.0 1.1 convolution_bitcast_fusion.1
  141.1 0.8 convolution_bitcast_fusion.10
  142.5 9.0 %scatter_custom_fusion.3 = f32[3,256]{0,1:T(8,128)S(1)} fusion(s32[1152]{0:T(1024)} %copy-done.35, f32[1152,3]{1,0:T(8,128)S(1)} %copy.157, f32[]{:T(128)} %constant.96.clone.1), kind=kCustom, calls=%fused_computation.125 | custom fusion | flops 3456 | bytes 3584 | tf_op jit(solution)/shard_map/transpose(jvp(jit(_take)))/scatter-add | solution.py:83
  151.8 3.6 %collective-permute-start.6 = (f32[3,1,8,4]{2,3,1,0:T(4,128)S(1)}, f32[3,1,8,4]{2,3,1,0:T(4,128)S(1)}, u32[]{:S(2)}, u32[]{:S(2)}) collective-permute-start(f32[3,1,8,4]{2,3,1,0:T(4,128)S(1)} %get-tuple-element.43), channel_id=1, source_target_pairs={{0,64},{64,128},{128,192},{192,256},{256,320},{320,384},{384,448},... | collective-permute-start | bytes 1160 | tf_op jit(solution)/shard_map/ppermute | solution.py:25
  155.4 2.5 collective-permute-start.7
  158.2 8.9 %scatter_custom_fusion.2 = f32[3,72]{0,1:T(8,128)S(1)} fusion(s32[1152]{0:T(1024)} %copy-done.34, f32[1152,3]{1,0:T(8,128)S(1)} %copy.156, f32[]{:T(128)} %constant.96.clone.1), kind=kCustom, calls=%fused_computation.154 | custom fusion | flops 3456 | bytes 1376 | tf_op jit(solution)/shard_map/transpose(jvp(jit(_take)))/scatter-add | solution.py:83
  167.5 1.9 collective-permute-start.8
  169.4 10.0 %collective-permute-start.9 = (f32[3,10,1,4]{2,3,1,0:T(4,128)S(1)}, f32[3,10,1,4]{2,3,1,0:T(4,128)S(1)}, u32[]{:S(2)}, u32[]{:S(2)}) collective-permute-start(f32[3,10,1,4]{2,3,1,0:T(4,128)S(1)} %get-tuple-element.42), channel_id=1, source_target_pairs={{8,0},{16,8},{24,16},{32,24},{40,32},{48,40},{56,48},{0,56},{9,1},... | collective-permute-start | bytes 1448 | tf_op jit(solution)/shard_map/ppermute | solution.py:28
  179.4 0.3 fusion.13
  179.8 99.2 %psum.7 = f32[3,3]{0,1:T(4,128)S(1)} all-reduce(f32[3,3]{0,1:T(4,128)S(1)} %fusion.13), channel_id=1, replica_groups=mesh['gx'=8,'gy'=8,'gz'=8] {'gx','gy','gz'}, use_global_device_ids=true, to_apply=%region_12.13 | all-reduce | flops 9 | bytes 72 | tf_op jit(solution)/shard_map/psum | solution.py:184
  279.2 1.9 collective-permute-start.10
  281.1 4.6 %collective-permute-start.11 = (f32[3,10,10,1]{2,3,1,0:T(1,128)S(1)}, f32[3,10,10,1]{2,3,1,0:T(1,128)S(1)}, u32[]{:S(2)}, u32[]{:S(2)}) collective-permute-start(f32[3,10,10,1]{2,3,1,0:T(1,128)S(1)} %get-tuple-element.38), channel_id=1, source_target_pairs={{1,0},{2,1},{3,2},{4,3},{5,4},{6,5},{7,6},{0,7},{9,8},{10,9},{11,1... | collective-permute-start | bytes 3608 | tf_op jit(solution)/shard_map/ppermute | solution.py:28
  285.7 9.8 %scatter_custom_fusion.5 = f32[72]{0:T(128)} fusion(s32[1152]{0:T(1024)} %copy-done.34, f32[1152]{0:T(1024)S(1)} %get-tuple-element.61, f32[]{:T(128)} %constant.96.clone.1), kind=kCustom, calls=%fused_computation.223 | custom fusion | flops 1152 | bytes 800 | tf_op jit(solution)/shard_map/jvp()/scatter-add | solution.py:111
  295.5 0.7 copy.164
  296.9 0.9 scatter_fusion
  297.8 0.6 copy.163
  (170 shorter events, 6.1 us)
Async XLA Ops:
  0.6 100.3 %copy-start = (f32[128,256]{1,0:T(8,128)S(1)}, f32[128,256]{1,0:T(8,128)}, u32[]{:S(2)}) copy-start(f32[128,256]{1,0:T(8,128)} %param.23) | copy-start | bytes 393220
  0.6 41.6 %copy-start.1 = (s32[1,72]{1,0:T(1,128)S(1)}, s32[1,72]{1,0:T(1,128)}, u32[]{:S(2)}) copy-start(s32[1,72]{1,0:T(1,128)} %param.14) | copy-start | bytes 868
  1.4 3.4 %copy-start.43 = (s32[72]{0:T(128)}, s32[72]{0:T(128)S(1)}, u32[]{:S(2)}) copy-start(s32[72]{0:T(128)S(1)} %fusion.91) | copy-start | bytes 868
  7.6 12.2 %collective-permute-start = (f32[4,1,6,2]{2,1,3,0:T(1,128)S(1)}, f32[4,1,6,2]{2,1,3,0:T(1,128)S(1)}, u32[]{:S(2)}, u32[]{:S(2)}) collective-permute-start(f32[4,1,6,2]{2,1,3,0:T(1,128)S(1)} %get-tuple-element.51), channel_id=1, source_target_pairs={{0,64},{64,128},{128,192},{192,256},{256,320},{320,384},{384,448},... | collective-permute-start | bytes 584 | tf_op jit(solution)/shard_map/ppermute | solution.py:25
  12.2 7.6 %collective-permute-start.1 = (f32[4,1,6,2]{2,1,3,0:T(1,128)S(1)}, f32[4,1,6,2]{2,1,3,0:T(1,128)S(1)}, u32[]{:S(2)}, u32[]{:S(2)}) collective-permute-start(f32[4,1,6,2]{2,1,3,0:T(1,128)S(1)} %get-tuple-element.52), channel_id=1, source_target_pairs={{64,0},{128,64},{192,128},{256,192},{320,256},{384,320},{448,384},... | collective-permute-start | bytes 584 | tf_op jit(solution)/shard_map/ppermute | solution.py:28
  19.0 61.9 %copy-start.34 = (s32[1152]{0:T(1024)}, s32[1152]{0:T(1024)S(1)}, u32[]{:S(2)}) copy-start(s32[1152]{0:T(1024)S(1)} %fusion.81) | copy-start | bytes 13828
  19.8 29.5 %copy-start.35 = (s32[1152]{0:T(1024)}, s32[1152]{0:T(1024)S(1)}, u32[]{:S(2)}) copy-start(s32[1152]{0:T(1024)S(1)} %fusion.82) | copy-start | bytes 13828
  19.8 51.4 %copy-start.41 = (f32[8]{0:T(128)}, f32[8]{0:T(128)S(1)}, u32[]{:S(2)}) copy-start(f32[8]{0:T(128)S(1)} %convert_multiply_fusion) | copy-start | bytes 100
  19.9 11.4 %collective-permute-start.2 = (f32[4,8,1,2]{2,1,3,0:T(8,128)S(1)}, f32[4,8,1,2]{2,1,3,0:T(8,128)S(1)}, u32[]{:S(2)}, u32[]{:S(2)}) collective-permute-start(f32[4,8,1,2]{2,1,3,0:T(8,128)S(1)} %get-tuple-element.49), channel_id=1, source_target_pairs={{0,8},{8,16},{16,24},{24,32},{32,40},{40,48},{48,56},{56,0},{1,9},... | collective-permute-start | bytes 776 | tf_op jit(solution)/shard_map/ppermute | solution.py:25
  21.8 10.4 %collective-permute-start.3 = (f32[4,8,1,2]{2,1,3,0:T(8,128)S(1)}, f32[4,8,1,2]{2,1,3,0:T(8,128)S(1)}, u32[]{:S(2)}, u32[]{:S(2)}) collective-permute-start(f32[4,8,1,2]{2,1,3,0:T(8,128)S(1)} %get-tuple-element.50), channel_id=1, source_target_pairs={{8,0},{16,8},{24,16},{32,24},{40,32},{48,40},{56,48},{0,56},{9,1},... | collective-permute-start | bytes 776 | tf_op jit(solution)/shard_map/ppermute | solution.py:28
  32.4 27.2 %collective-permute-start.4 = (f32[4,8,8,1]{2,1,3,0:T(8,128)S(1)}, f32[4,8,8,1]{2,1,3,0:T(8,128)S(1)}, u32[]{:S(2)}, u32[]{:S(2)}) collective-permute-start(f32[4,8,8,1]{2,1,3,0:T(8,128)S(1)} %get-tuple-element.47), channel_id=1, source_target_pairs={{0,1},{1,2},{2,3},{3,4},{4,5},{5,6},{6,7},{7,0},{8,9},{9,10},{10,1... | collective-permute-start | bytes 3080 | tf_op jit(solution)/shard_map/ppermute | solution.py:25
  34.3 25.3 %collective-permute-start.5 = (f32[4,8,8,1]{2,1,3,0:T(8,128)S(1)}, f32[4,8,8,1]{2,1,3,0:T(8,128)S(1)}, u32[]{:S(2)}, u32[]{:S(2)}) collective-permute-start(f32[4,8,8,1]{2,1,3,0:T(8,128)S(1)} %get-tuple-element.48), channel_id=1, source_target_pairs={{1,0},{2,1},{3,2},{4,3},{5,4},{6,5},{7,6},{0,7},{9,8},{10,9},{11,1... | collective-permute-start | bytes 3080 | tf_op jit(solution)/shard_map/ppermute | solution.py:28
  59.3 11.3 %copy-start.27 = (f32[1152]{0:T(1024)}, f32[1152]{0:T(1024)S(1)}, u32[]{:S(2)}) copy-start(f32[1152]{0:T(1024)S(1)} %gather_fusion.7) | copy-start | bytes 13828
  59.9 7.3 %copy-start.36 = (s32[1,1152]{1,0:T(1,128)S(1)}, s32[1,1152]{1,0:T(1,128)}, u32[]{:S(2)}) copy-start(s32[1,1152]{1,0:T(1,128)} %param.16) | copy-start | bytes 13828
  59.9 7.3 %copy-start.37 = (s32[1,1152]{1,0:T(1,128)S(1)}, s32[1,1152]{1,0:T(1,128)}, u32[]{:S(2)}) copy-start(s32[1,1152]{1,0:T(1,128)} %param.17) | copy-start | bytes 13828
  59.9 12.1 %copy-start.38 = (f32[128,16]{0,1:T(8,128)S(1)}, f32[128,16]{0,1:T(8,128)}, u32[]{:S(2)}) copy-start(f32[128,16]{0,1:T(8,128)} %param.19) | copy-start | bytes 24580
  60.0 13.2 %copy-start.32 = (f32[64,128]{1,0:T(8,128)S(1)}, f32[64,128]{1,0:T(8,128)}, u32[]{:S(2)}) copy-start(f32[64,128]{1,0:T(8,128)} %param.20) | copy-start | bytes 98308
  67.3 6.8 %copy-start.18 = (f32[64,64]{1,0:T(8,128)S(1)}, f32[64,64]{1,0:T(8,128)}, u32[]{:S(2)}) copy-start(f32[64,64]{1,0:T(8,128)} %param.22) | copy-start | bytes 49156
  67.3 8.0 %copy-start.19 = (f32[64,64]{1,0:T(8,128)S(1)}, f32[64,64]{1,0:T(8,128)}, u32[]{:S(2)}) copy-start(f32[64,64]{1,0:T(8,128)} %param.21) | copy-start | bytes 49156
  67.4 31.7 %copy-start.29 = (pred[1152]{0:T(1024)(128)(4,1)}, pred[1152]{0:T(1024)(128)(4,1)S(1)}, u32[]{:S(2)}) copy-start(pred[1152]{0:T(1024)(128)(4,1)S(1)} %compare_and_fusion.2) | copy-start | bytes 3460
  67.8 7.4 %copy-start.8 = (f32[3,8,8,4]{0,3,2,1:T(4,128)}, f32[3,8,8,4]{0,3,2,1:T(4,128)S(1)}, u32[]{:S(2)}) copy-start(f32[3,8,8,4]{0,3,2,1:T(4,128)S(1)} %copy.148) | copy-start | bytes 9220
  70.6 0.7 copy-start.23
  71.2 0.6 copy-start.25
  71.2 6.9 %copy-start.21 = (f32[1152]{0:T(1024)}, f32[1152]{0:T(1024)S(1)}, u32[]{:S(2)}) copy-start(f32[1152]{0:T(1024)S(1)} %get-tuple-element.65) | copy-start | bytes 13828
  73.1 5.0 %copy-start.15 = (f32[128,1152]{0,1:T(8,128)}, f32[128,1152]{0,1:T(8,128)S(1)}, u32[]{:S(2)}) copy-start(f32[128,1152]{0,1:T(8,128)S(1)} %convolution_bitcast_fusion.4) | copy-start | bytes 1769476
  74.1 4.1 %copy-start.12 = (f32[1152,64]{0,1:T(8,128)}, f32[1152,64]{0,1:T(8,128)S(1)}, u32[]{:S(2)}) copy-start(f32[1152,64]{0,1:T(8,128)S(1)} %fusion.26) | copy-start | bytes 884740
  76.3 1.8 copy-start.3
  99.1 1.0 copy-start.7
  100.1 3.2 %copy-start.2 = (f32[9,64,1152]{2,1,0:T(8,128)}, f32[9,64,1152]{2,1,0:T(8,128)S(1)}, u32[]{:S(2)}) copy-start(f32[9,64,1152]{2,1,0:T(8,128)S(1)} %select_multiply_fusion) | copy-start | bytes 7962628
  100.1 1.2 copy-start.13
  100.1 3.2 %copy-start.31 = (f32[64,128]{1,0:T(8,128)S(1)}, f32[64,128]{1,0:T(8,128)}, u32[]{:S(2)}) copy-start(f32[64,128]{1,0:T(8,128)} %param.24) | copy-start | bytes 98308
  100.9 4.0 %copy-start.30 = (f32[1152]{0:T(1024)S(1)}, f32[1152]{0:T(1024)}, u32[]{:S(2)}) copy-start(f32[1152]{0:T(1024)} %get-tuple-element.63) | copy-start | bytes 13828
  100.9 4.0 %copy-start.45 = (f32[64]{0:T(128)S(1)}, f32[64]{0:T(128)}, u32[]{:S(2)}) copy-start(f32[64]{0:T(128)} %param.25) | copy-start | bytes 772
  106.9 1.1 copy-start.14
  108.0 0.7 copy-start.6
  108.0 2.3 copy-start.5
  130.2 3.5 %copy-start.4 = (f32[64,1152]{1,0:T(8,128)S(1)}, f32[64,1152]{1,0:T(8,128)}, u32[]{:S(2)}) copy-start(f32[64,1152]{1,0:T(8,128)} %copy-done.3) | copy-start | bytes 884740
  133.7 3.3 %copy-start.17 = (f32[64,1152]{1,0:T(8,128)S(1)}, f32[64,1152]{1,0:T(8,128)}, u32[]{:S(2)}) copy-start(f32[64,1152]{1,0:T(8,128)} %convolution_bitcast_fusion.9) | copy-start | bytes 884740
  133.7 3.3 %copy-start.46 = (f32[64]{0:T(128)S(1)}, f32[64]{0:T(128)}, u32[]{:S(2)}) copy-start(f32[64]{0:T(128)} %param.25) | copy-start | bytes 772
  133.7 3.6 %copy-start.10 = (f32[64,1152]{1,0:T(8,128)S(1)}, f32[64,1152]{1,0:T(8,128)}, u32[]{:S(2)}) copy-start(f32[64,1152]{1,0:T(8,128)} %get-tuple-element.29) | copy-start | bytes 884740
  133.7 5.6 %copy-start.11 = (f32[64,1152]{1,0:T(8,128)S(1)}, f32[64,1152]{1,0:T(8,128)}, u32[]{:S(2)}) copy-start(f32[64,1152]{1,0:T(8,128)} %get-tuple-element.67) | copy-start | bytes 884740
  133.7 5.7 %copy-start.20 = (f32[64,64]{1,0:T(8,128)S(1)}, f32[64,64]{1,0:T(8,128)}, u32[]{:S(2)}) copy-start(f32[64,64]{1,0:T(8,128)} %param.21) | copy-start | bytes 49156
  133.7 5.7 %copy-start.22 = (f32[1152]{0:T(1024)S(1)}, f32[1152]{0:T(1024)}, u32[]{:S(2)}) copy-start(f32[1152]{0:T(1024)} %copy-done.21) | copy-start | bytes 13828
  136.8 3.2 %copy-start.33 = (f32[64,128]{1,0:T(8,128)S(1)}, f32[64,128]{1,0:T(8,128)}, u32[]{:S(2)}) copy-start(f32[64,128]{1,0:T(8,128)} %param.20) | copy-start | bytes 98308
  136.8 4.3 %copy-start.16 = (f32[128,1152]{0,1:T(8,128)S(1)}, f32[128,1152]{0,1:T(8,128)}, u32[]{:S(2)}) copy-start(f32[128,1152]{0,1:T(8,128)} %copy-done.15) | copy-start | bytes 1769476
  136.8 4.3 %copy-start.39 = (f32[128,16]{0,1:T(8,128)S(1)}, f32[128,16]{0,1:T(8,128)}, u32[]{:S(2)}) copy-start(f32[128,16]{0,1:T(8,128)} %param.19) | copy-start | bytes 24580
  139.4 2.5 copy-start.26
  139.5 2.5 copy-start.42
  139.5 2.7 copy-start.24
  139.5 2.7 copy-start.28
  141.1 38.3 %copy-start.9 = (f32[3,8,8,4]{0,3,2,1:T(4,128)S(1)}, f32[3,8,8,4]{0,3,2,1:T(4,128)}, u32[]{:S(2)}) copy-start(f32[3,8,8,4]{0,3,2,1:T(4,128)} %copy-done.8) | copy-start | bytes 9220
  141.1 155.2 %copy-start.40 = (pred[6]{0:T(512)(128)(4,1)S(1)}, pred[6]{0:T(512)(128)(4,1)}, u32[]{:S(2)}) copy-start(pred[6]{0:T(512)(128)(4,1)} %constant.165.clone.1) | copy-start | bytes 22
  142.0 154.7 %copy-start.47 = (pred[2]{0:T(512)(128)(4,1)S(1)}, pred[2]{0:T(512)(128)(4,1)}, u32[]{:S(2)}) copy-start(pred[2]{0:T(512)(128)(4,1)} %constant.166.clone.1) | copy-start | bytes 10
  142.0 154.9 %copy-start.44 = (s32[72]{0:T(128)S(1)}, s32[72]{0:T(128)}, u32[]{:S(2)}) copy-start(s32[72]{0:T(128)} %copy-done.43) | copy-start | bytes 868
  151.8 15.5 %collective-permute-start.6 = (f32[3,1,8,4]{2,3,1,0:T(4,128)S(1)}, f32[3,1,8,4]{2,3,1,0:T(4,128)S(1)}, u32[]{:S(2)}, u32[]{:S(2)}) collective-permute-start(f32[3,1,8,4]{2,3,1,0:T(4,128)S(1)} %get-tuple-element.43), channel_id=1, source_target_pairs={{0,64},{64,128},{128,192},{192,256},{256,320},{320,384},{384,448},... | collective-permute-start | bytes 1160 | tf_op jit(solution)/shard_map/ppermute | solution.py:25
  155.4 12.0 %collective-permute-start.7 = (f32[3,1,8,4]{2,3,1,0:T(4,128)S(1)}, f32[3,1,8,4]{2,3,1,0:T(4,128)S(1)}, u32[]{:S(2)}, u32[]{:S(2)}) collective-permute-start(f32[3,1,8,4]{2,3,1,0:T(4,128)S(1)} %get-tuple-element.44), channel_id=1, source_target_pairs={{64,0},{128,64},{192,128},{256,192},{320,256},{384,320},{448,384},... | collective-permute-start | bytes 1160 | tf_op jit(solution)/shard_map/ppermute | solution.py:28
  167.5 111.5 %collective-permute-start.8 = (f32[3,10,1,4]{2,3,1,0:T(4,128)S(1)}, f32[3,10,1,4]{2,3,1,0:T(4,128)S(1)}, u32[]{:S(2)}, u32[]{:S(2)}) collective-permute-start(f32[3,10,1,4]{2,3,1,0:T(4,128)S(1)} %get-tuple-element.41), channel_id=1, source_target_pairs={{0,8},{8,16},{16,24},{24,32},{32,40},{40,48},{48,56},{56,0},{1,9},... | collective-permute-start | bytes 1448 | tf_op jit(solution)/shard_map/ppermute | solution.py:25
  169.4 109.5 %collective-permute-start.9 = (f32[3,10,1,4]{2,3,1,0:T(4,128)S(1)}, f32[3,10,1,4]{2,3,1,0:T(4,128)S(1)}, u32[]{:S(2)}, u32[]{:S(2)}) collective-permute-start(f32[3,10,1,4]{2,3,1,0:T(4,128)S(1)} %get-tuple-element.42), channel_id=1, source_target_pairs={{8,0},{16,8},{24,16},{32,24},{40,32},{48,40},{56,48},{0,56},{9,1},... | collective-permute-start | bytes 1448 | tf_op jit(solution)/shard_map/ppermute | solution.py:28
  279.2 17.0 %collective-permute-start.10 = (f32[3,10,10,1]{2,3,1,0:T(1,128)S(1)}, f32[3,10,10,1]{2,3,1,0:T(1,128)S(1)}, u32[]{:S(2)}, u32[]{:S(2)}) collective-permute-start(f32[3,10,10,1]{2,3,1,0:T(1,128)S(1)} %get-tuple-element.37), channel_id=1, source_target_pairs={{0,1},{1,2},{2,3},{3,4},{4,5},{5,6},{6,7},{7,0},{8,9},{9,10},{10,1... | collective-permute-start | bytes 3608 | tf_op jit(solution)/shard_map/ppermute | solution.py:25
  281.1 15.1 %collective-permute-start.11 = (f32[3,10,10,1]{2,3,1,0:T(1,128)S(1)}, f32[3,10,10,1]{2,3,1,0:T(1,128)S(1)}, u32[]{:S(2)}, u32[]{:S(2)}) collective-permute-start(f32[3,10,10,1]{2,3,1,0:T(1,128)S(1)} %get-tuple-element.38), channel_id=1, source_target_pairs={{1,0},{2,1},{3,2},{4,3},{5,4},{6,5},{7,6},{0,7},{9,8},{10,9},{11,1... | collective-permute-start | bytes 3608 | tf_op jit(solution)/shard_map/ppermute | solution.py:28
where the time goes:
time: 300 us; the launch traced here: 298 us
  blocking collectives  99.2 us (33%)
  other arithmetic  65.2 us (22%)
  local copies, waits for them, and re-layouts  59.1 us (20%)
  starting transfers between devices  56.4 us (19%)
  matrix products  15.2 us (5%)
    psum x1, blocking collectives, body(): virial = lax.psum(virial_part, ('gx', 'gy', 'gz')) * normalizer  99.2 us
    ppermute x6, starting transfers between devices, extended_2(): lax.ppermute(lax.slice_in_dim(block, 0, width, axis=dim), axis, backward)  40.5 us
    ppermute x6, starting transfers between devices, extended_2(): lax.ppermute(lax.slice_in_dim(block, block.shape[dim] - width, None, axis...  15.8 us
    dot_general x15, matrix products, matmul(): jnp.dot(left, right, precision=highest, preferred_element_type=jnp.float32)  15.2 us
    scatter-add x1, other arithmetic, domain_energy(): jnp.take(environment, center, axis=1).reshape(9, channels, edge_total)  11.6 us
    scatter-add x1, other arithmetic, domain_energy(): jnp.zeros((9 * channels, atom_count), jnp.float32).at[:, center]  10.9 us
    scatter-add x1, other arithmetic, domain_energy(): return jnp.zeros((atom_count,), jnp.float32).at[center].add(edge_energy)  9.81 us
    scatter-add x1, other arithmetic, domain_energy(): jnp.take(extended_pos, partner, axis=1)  8.99 us
  transfers between devices with their start and end apart: 12, of which 2 were waited for; matrix products, arithmetic and copies ran while one was open for 13% of the time, Pallas kernels for 0%

commit v1 on v0

v1 whole, which is shorter than its diff:
```python
import math

import jax
import jax.numpy as jnp
import numpy as np
from jax import lax
from jax.experimental import pallas as pl
from jax.experimental.pallas import tpu as pltpu
from jax.sharding import PartitionSpec as P

CELLS = 6
LAYERS = 2
ATOMS = 72
EDGES = 1152
BLOCKS = 9
LANES = 128
MAIN = 64
COUNT = 8
F32 = jnp.float32
BF16 = jnp.bfloat16
HIGHEST = lax.Precision.HIGHEST
ROOT3 = math.sqrt(3.0)
RING = 28
STEPS = [(dx, dy) for dx in (-1, 0, 1) for dy in (-1, 0, 1) if (dx, dy) != (0, 0)]


RIM_SITES = (
    [(0, y) for y in range(6)]
    + [(5, y) for y in range(6)]
    + [(x, 0) for x in range(1, 5)]
    + [(x, 5) for x in range(1, 5)]
)


def ring_index(i, j):
    if i == 0:
        return j
    if i == 7:
        return 8 + j
    if j == 0:
        return 16 + i - 1
    return 22 + i - 1


def cell_number(i, j, k):
    if i in (0, 7) or j in (0, 7):
        return k * RING + ring_index(i, j)
    return 112 + k * 36 + (i - 1) * 6 + (j - 1)


def tables():
    forward = np.zeros((10 * LANES, 256), np.float32)
    for n, (dx, dy) in enumerate(STEPS):
        for m, (x, y) in enumerate(RIM_SITES):
            i = {0: x + 1, 1: 7 if x == 0 else None, -1: 0 if x == 5 else None}[dx]
            j = {0: y + 1, 1: 7 if y == 0 else None, -1: 0 if y == 5 else None}[dy]
            if i is None or j is None:
                continue
            for k in range(4):
                forward[n * LANES + k * 32 + m, cell_number(i, j, k)] = 1.0
    for x in range(CELLS):
        for y in range(CELLS):
            for k, at in ((0, 0), (3, 64), (1, LANES), (2, LANES + 64)):
                forward[8 * LANES + at + x * 6 + y, cell_number(x + 1, y + 1, k)] = 1.0
    back = np.zeros((10 * LANES, 256), np.float32)
    places = {0: 0, 3: 64, 1: LANES, 2: LANES + 64}
    for n, (dx, dy) in enumerate(STEPS):
        for i in range(8):
            for j in range(8):
                if not (i in (0, 7) or j in (0, 7)):
                    continue
                x, y = dx * 6 + i - 1, dy * 6 + j - 1
                if 0 <= x < 6 and 0 <= y < 6:
                    for k in range(4):
                        back[n * LANES + cell_number(i, j, k), places[k] + x * 6 + y] = 1.0
    for x in range(CELLS):
        for y in range(CELLS):
            for k in range(4):
                back[8 * LANES + cell_number(x + 1, y + 1, k), places[k] + x * 6 + y] = 1.0
    return forward, back


FORWARD, BACK = tables()


def parts_of(x, count):
    found = []
    for _ in range(count - 1):
        part = x.astype(BF16).astype(F32)
        found.append(part)
        x = x - part
    found.append(x)
    return found


def split_rows(x, count):
    return jnp.concatenate(parts_of(x, count), axis=0).astype(BF16)


def exact_dot(x, table, count=3):
    rows = x.shape[0]
    out = jnp.dot(split_rows(x, count), table, preferred_element_type=F32)
    return sum(out[i * rows : (i + 1) * rows] for i in range(1, count)) + out[:rows]


def exact_dot_nt(x, table, count=3):
    rows = x.shape[0]
    out = lax.dot_general(split_rows(x, count), table, (((1,), (1,)), ((), ())), preferred_element_type=F32)
    return sum(out[i * rows : (i + 1) * rows] for i in range(1, count)) + out[:rows]


def pad_rows(x):
    return jnp.concatenate([x, jnp.zeros((8 - x.shape[0], x.shape[1]), F32)], axis=0)


def iota(shape, dim):
    return lax.broadcasted_iota(jnp.int32, shape, dim)


def as_hot(mask):
    return jnp.where(mask, 1.0, 0.0).astype(BF16)


def fetch(sources, buffers, sems):
    copies = [pltpu.make_async_copy(src, dst, sems.at[n]) for n, (src, dst) in enumerate(zip(sources, buffers))]
    for copy in copies:
        copy.start()
    for copy in copies:
        copy.wait()


def atom_rows(pos_ref, kind_ref):
    kind = kind_ref[...].astype(F32)
    return jnp.concatenate([pos_ref[0], pos_ref[1], pos_ref[2], kind, jnp.zeros((4, ATOMS), F32)], axis=0)


def lane_sites():
    lane = iota((8, 3 * LANES), 1)
    part, at = lane >> 7, lane & 63
    second = (lane & 64) > 0
    rim = jnp.where(
        at < 12,
        jnp.where(at < 6, at, 24 + at),
        jnp.where(at < 16, 6 * (at - 11), 6 * (at - 15) + 5),
    )
    whole = jnp.where(at < 36, at, 1000)
    rim = jnp.where(at < 20, rim, 1000)
    layer = jnp.where(part == 0, jnp.where(second, 1, 0), part - 1)
    return 2 * jnp.where((part > 0) & second, rim, whole) + layer


def send_kernel(pos_hbm, kind_hbm, site_hbm, own_ref, down_ref, up_ref, hot_ref, pos_ref, kind_ref, site_ref, sems):
    fetch((pos_hbm, kind_hbm, site_hbm), (pos_ref, kind_ref, site_ref), sems)
    rows = atom_rows(pos_ref, kind_ref)
    hot = as_hot(iota((ATOMS, ATOMS), 0) == site_ref[...])
    pick = as_hot(iota((ATOMS, 3 * LANES), 0) == lane_sites()[0:1])
    placed = jnp.dot(hot, pick, preferred_element_type=F32).astype(BF16)
    out = exact_dot(rows, placed)
    own_ref[...] = out[:4, 0:LANES]
    down_ref[...] = out[:4, LANES : 2 * LANES]
    up_ref[...] = out[:4, 2 * LANES : 3 * LANES]
    hot_ref[...] = placed[:, 0:LANES]


def column_kernel(down_ref, up_ref, below_ref, above_ref, tie_ref, msg_ref, outer_ref):
    lane = lax.broadcasted_iota(jnp.int32, (8, LANES), 1)

    def rim(x, at):
        return pltpu.roll(x, (at - 64) % LANES, 1)

    below, above, low, high = (pad_rows(ref[...]) for ref in (below_ref, above_ref, down_ref, up_ref))
    msg = jnp.where(
        lane < 32,
        rim(below, 0),
        jnp.where(lane < 64, rim(low, 32), jnp.where(lane < 96, rim(high, 64), rim(above, 96))),
    )
    outer_ref[...] = jnp.where(lane < 64, below, pltpu.roll(above, 64, 1))[:4]
    msg_ref[...] = jnp.broadcast_to(msg[:4][None], (COUNT * COUNT, 4, LANES))


def cat_of(w):
    high = w.astype(BF16).astype(F32)
    low = w - high
    return jnp.concatenate([high, high, low], axis=1).astype(BF16)


def cell_shifts():
    lane = iota((8, 256), 1)
    row = iota((8, 256), 0)
    inside = lane - 112
    ring_layer = jnp.where(lane >= 28, 1, 0) + jnp.where(lane >= 56, 1, 0) + jnp.where(lane >= 84, 1, 0)
    ring = lane - 28 * ring_layer
    outer = lane < 112
    layer = jnp.where(
        outer,
        ring_layer,
        jnp.where(inside >= 36, 1, 0) + jnp.where(inside >= 72, 1, 0) + jnp.where(inside >= 108, 1, 0),
    )
    low_z = layer == 0
    high_z = layer == 3
    corner_low = (ring == 0) | (ring == 8)
    corner_high = (ring == 7) | (ring == 15)
    low_y = outer & (corner_low | ((ring >= 16) & (ring < 22)))
    high_y = outer & (corner_high | (ring >= 22))
    low_x = outer & (ring < 8)
    high_x = outer & (ring >= 8) & (ring < 16)

    def sides(low, high, edge):
        return jnp.where(high, edge, 0.0) - jnp.where(low, edge, 0.0)

    return jnp.where(
        row == 0,
        sides(low_x, high_x, 12.0),
        jnp.where(row == 1, sides(low_y, high_y, 12.0), jnp.where(row == 2, sides(low_z, high_z, 4.0), 0.0)),
    )


def prepare_kernel(count_ref, *refs):
    sources, outputs, buffers, sems = refs[:13], refs[13:26], refs[26:37], refs[37]
    cell_ref, live_ref, own_ref, shift_ref = outputs[:4]
    win_ref, w3_ref, wlat_ref, wlat_t_ref, w3_t_ref, win_t_ref, read_ref = outputs[4:11]
    fetch(sources, buffers + outputs[11:], sems)
    center_ref, other_ref, pos_ref, kind_ref, w_in_ref, w_two_ref, w_env_ref = buffers[:7]
    w_value_ref, w_latent_ref, w_out_ref, readout_ref = buffers[7:]
    shift_ref[...] = cell_shifts()
    before = as_hot((iota((LANES, 256), 0) < iota((LANES, 256), 1)) | (iota((LANES, 256), 1) >= LANES))
    lane = iota((ATOMS, 256), 1)
    spread = as_hot(iota((ATOMS, 256), 0) == jnp.where(lane < LANES, lane & 63, MAIN + (lane & 7)))
    center = center_ref[...]
    other = other_ref[...]
    atom = lax.broadcasted_iota(jnp.int32, (ATOMS, EDGES), 0)
    hot = jnp.where(atom == center, 1.0, 0.0)
    hot16 = hot.astype(BF16)
    running = jnp.zeros((ATOMS, LANES), F32)
    ranks = []
    for b in range(BLOCKS):
        at = slice(b * LANES, (b + 1) * LANES)
        sums = jnp.dot(hot16[:, at], before, preferred_element_type=F32)
        ranks.append(jnp.sum(hot[:, at] * (sums[:, :LANES] + running), axis=0, keepdims=True))
        running = running + sums[:, LANES:]
    rank = jnp.concatenate(ranks, axis=1).astype(jnp.int32)
    is_main = center < MAIN
    block = jnp.where(is_main, rank >> 1, BLOCKS - 1)
    lane = jnp.where(is_main, (rank & 1) * MAIN + center, rank * 8 + (center - MAIN))
    i, j, k = other >> 5, (other >> 2) & 7, other & 3
    ring = jnp.where(
        i == 0, j, jnp.where(i == 7, 8 + j, jnp.where(j == 0, 15 + i, jnp.where(j == 7, 21 + i, -1)))
    )
    cell = jnp.where(ring >= 0, k * RING + ring, 112 + k * 36 + (i - 1) * 6 + (j - 1)).astype(F32)
    slot = lax.broadcasted_iota(jnp.int32, (1, EDGES), 1)
    live = jnp.where(slot < count_ref[0], 1.0, 0.0)
    row = lax.broadcasted_iota(jnp.int32, (16, EDGES), 0)
    left = jnp.concatenate([jnp.where(row == block, cell, 0.0), jnp.where(row == block, live, 0.0)], axis=0)
    lane_hot = jnp.where(lax.broadcasted_iota(jnp.int32, (LANES, EDGES), 0) == lane, 1.0, 0.0).astype(BF16)
    placed = lax.dot_general(
        left.astype(BF16), lane_hot, (((1,), (1,)), ((), ())), preferred_element_type=F32
    )
    for b in range(BLOCKS):
        at = slice(b * LANES, (b + 1) * LANES)
        cell_ref[:, at] = placed[b : b + 1].astype(jnp.int32)
        live_ref[:, at] = placed[16 + b : 17 + b]
    own_ref[...] = exact_dot(atom_rows(pos_ref, kind_ref), spread)

    w_in_t = w_in_ref[...]
    win_ref[...] = cat_of(w_in_t.T)
    w_two = w_two_ref[...]
    mixed = jnp.concatenate([w_env_ref[...], w_value_ref[...]], axis=0)
    w3 = jnp.concatenate(
        [w_two, jnp.dot(mixed, w_two, precision=HIGHEST, preferred_element_type=F32)], axis=0
    )
    w3_ref[...] = cat_of(w3)
    w3_t_ref[...] = cat_of(w3.T)
    w_latent = w_latent_ref[...]
    wlat_ref[...] = cat_of(w_latent)
    wlat_t_ref[...] = cat_of(w_latent.T)
    win_t_ref[...] = cat_of(w_in_t)
    square = lax.broadcasted_iota(jnp.int32, (64, 64), 0) == lax.broadcasted_iota(jnp.int32, (64, 64), 1)
    column = jnp.sum(jnp.where(square, readout_ref[...], 0.0), axis=1, keepdims=True)
    read_ref[...] = jnp.dot(
        w_out_ref[...].T,
        jnp.broadcast_to(column, (64, LANES)),
        precision=HIGHEST,
        preferred_element_type=F32,
    )


def cos_sin_pi(t):
    whole = jnp.floor(t + 0.5)
    f = t - whole
    half = whole * 0.5
    sign = 1.0 - 4.0 * (half - jnp.floor(half))
    a = f * math.pi
    q = a * a
    c = 1.0 + q * (
        -0.5
        + q * (1 / 24 + q * (-1 / 720 + q * (1 / 40320 + q * (-1 / 3628800 + q * (1 / 479001600)))))
    )
    s = a * (
        1.0
        + q
        * (-1 / 6 + q * (1 / 120 + q * (-1 / 5040 + q * (1 / 362880 + q * (-1 / 39916800 + q * (1 / 6227020800))))))
    )
    return c * sign, s * sign


def sum_slots(main, last):
    main = main + pltpu.roll(main, 64, 1)
    for shift in (64, 32, 16, 8):
        last = last + pltpu.roll(last, shift, 1)
    return main, last


def store_cat(ref, row, depth, at, x):
    high = x.astype(BF16)
    low = (x - high.astype(F32)).astype(BF16)
    ref[pl.ds(pl.multiple_of(row, 16), 16), at] = high
    ref[pl.ds(pl.multiple_of(depth + row, 16), 16), at] = low
    ref[pl.ds(pl.multiple_of(2 * depth + row, 16), 16), at] = high


def neighbour(n):
    dx, dy = STEPS[n]
    gx = lax.axis_index("gx")
    gy = lax.axis_index("gy")
    return lax.rem(gx + (dx + COUNT), COUNT) * COUNT + lax.rem(gy + (dy + COUNT), COUNT)


def main_kernel(
    recv_ref,
    outer_ref,
    inner_ref,
    cell_ref,
    live_ref,
    own_ref,
    shift_ref,
    win_ref,
    w3_ref,
    wlat_ref,
    wlat_t_ref,
    w3_t_ref,
    win_t_ref,
    read_ref,
    forward_ref,
    msg_ref,
    ext_ref,
    local_ref,
    energy_ref,
    hot,
    harm,
    env_live,
    pre,
    slope,
    cat_a,
    cat_b,
    mixed,
    paths,
    environment,
    grad_lat,
    grad_harm,
    grad_env,
    energy,
):
    blocks = [slice(b * LANES, (b + 1) * LANES) for b in range(BLOCKS)]

    columns = [recv_ref[neighbour(n)] for n in range(8)] + [outer_ref[...], inner_ref[...]]
    arrived = pad_rows(jnp.concatenate(columns, axis=1))
    extended = exact_dot(arrived, forward_ref[...]) + shift_ref[...]
    cells = lax.broadcasted_iota(jnp.int32, (256, EDGES), 0)
    hot[...] = jnp.where(cells == cell_ref[...], 1.0, 0.0).astype(BF16)
    partner = exact_dot(extended, hot[...])
    own = own_ref[...]
    center = jnp.concatenate([own[:, :LANES]] * 8 + [own[:, LANES:]], axis=1)
    displacement = partner - center

    def wide(x, row):
        return jnp.broadcast_to(x[row : row + 1], (8, EDGES))

    x = wide(displacement, 0) * 0.2
    y = wide(displacement, 1) * 0.2
    z = wide(displacement, 2) * 0.2
    scaled = x * x + y * y + z * z
    live = jnp.broadcast_to(live_ref[...], (8, EDGES))
    env_live[...] = (1.0 - scaled) * (1.0 - scaled) * live
    harm[0] = x
    harm[1] = y
    harm[2] = z
    harm[3] = ROOT3 * x * y
    harm[4] = ROOT3 * y * z
    harm[5] = ROOT3 * x * z
    harm[6] = (0.5 * ROOT3) * (x * x - y * y)
    harm[7] = 0.5 * (2.0 * z * z - x * x - y * y)

    order = lax.broadcasted_iota(jnp.int32, (8, EDGES), 0)
    orders = order.astype(F32)
    radial, radial_sin = cos_sin_pi(orders * scaled)
    kinds = jnp.where(order < 4, wide(center, 3), wide(partner, 3) + 4.0)
    one_hot = jnp.where(kinds == orders, 1.0, 0.0)
    inputs = jnp.concatenate([radial, one_hot], axis=0)
    inputs_high = inputs.astype(BF16)
    inputs_low = (inputs - inputs_high.astype(F32)).astype(BF16)
    pre[0:16] = jnp.dot(
        win_ref[...],
        jnp.concatenate([inputs_high, inputs_low, inputs_high], axis=0),
        preferred_element_type=F32,
    ).reshape(16, 8, EDGES)

    def first_layer(c, carry):
        v = pre[pl.ds(2 * c, 2)]
        gate = 1.0 / (1.0 + jnp.exp(-v))
        out = v * gate
        slope[pl.ds(2 * c, 2)] = gate + out * (1.0 - gate)
        store_cat(cat_a, 16 * c, 128, slice(None), out.reshape(16, EDGES))
        return carry

    lax.fori_loop(0, 8, first_layer, 0)
    mixed[...] = jnp.dot(w3_ref[...], cat_a[0:384], preferred_element_type=F32).reshape(24, 8, EDGES)

    def forward_tile(t, carry):
        sums = [[None, None] for _ in range(9)]
        for b, at in enumerate(blocks):
            weight = mixed[pl.ds(8 + 2 * t, 2), :, at] * env_live[:, at]
            part = 0 if b < 8 else 1
            for r in range(9):
                term = weight if r == 0 else weight * harm[r - 1, :, at]
                sums[r][part] = term if sums[r][part] is None else sums[r][part] + term
        found = []
        for r in range(9):
            main, last = sum_slots(sums[r][0].reshape(16, LANES), sums[r][1].reshape(16, LANES))
            main, last = main.reshape(2, 8, LANES), last.reshape(2, 8, LANES)
            environment[r, pl.ds(2 * t, 2), :, 0:LANES] = main
            environment[r, pl.ds(2 * t, 2), :, LANES : 2 * LANES] = last
            found.append((main, last))
        for b, at in enumerate(blocks):
            part = 0 if b < 8 else 1
            h = [None] + [harm[r, :, at] for r in range(8)]
            e = [found[r][part] for r in range(9)]
            one = h[1] * e[1] + h[2] * e[2] + h[3] * e[3]
            two = h[4] * e[4] + h[5] * e[5] + h[6] * e[6] + h[7] * e[7] + h[8] * e[8]
            paths[0, pl.ds(2 * t, 2), :, at] = one
            paths[1, pl.ds(2 * t, 2), :, at] = two
            values = mixed[pl.ds(16 + 2 * t, 2), :, at]
            base = 16 * t
            store_cat(cat_b, base, 256, at, mixed[pl.ds(2 * t, 2), :, at].reshape(16, LANES))
            store_cat(cat_b, 64 + base, 256, at, (e[0] * values).reshape(16, LANES))
            store_cat(cat_b, 128 + base, 256, at, (one * values).reshape(16, LANES))
            store_cat(cat_b, 192 + base, 256, at, (two * values).reshape(16, LANES))
        return carry

    lax.fori_loop(0, 4, forward_tile, 0)
    pre[...] = jnp.dot(wlat_ref[...], cat_b[...], preferred_element_type=F32).reshape(16, 8, EDGES)
    energy[...] = jnp.zeros((8, EDGES), F32)

    def second_layer(c, carry):
        v = pre[pl.ds(2 * c, 2)]
        gate = 1.0 / (1.0 + jnp.exp(-v))
        out = v * gate
        weights = read_ref[pl.ds(pl.multiple_of(16 * c, 16), 16), :].reshape(2, 8, LANES)
        weights = jnp.concatenate([weights] * BLOCKS, axis=2)
        product = weights * out
        energy[...] += product[0] + product[1]
        back = weights * (gate + out * (1.0 - gate)) * env_live[...]
        store_cat(cat_a, 16 * c, 128, slice(None), back.reshape(16, EDGES))
        return carry

    lax.fori_loop(0, 8, second_layer, 0)
    grad_lat[...] = jnp.dot(wlat_t_ref[...], cat_a[...], preferred_element_type=F32).reshape(32, 8, EDGES)
    grad_harm[...] = jnp.zeros((8, 8, EDGES), F32)
    grad_env[...] = jnp.zeros((8, EDGES), F32)

    def backward_tile(t, carry):
        base = 16 * t
        sums = [[None, None] for _ in range(9)]
        for b, at in enumerate(blocks):
            part = 0 if b < 8 else 1
            lanes = slice(part * LANES, (part + 1) * LANES)
            values = mixed[pl.ds(16 + 2 * t, 2), :, at]
            d = [grad_lat[pl.ds(8 + 8 * l + 2 * t, 2), :, at] for l in range(3)]
            zero = environment[0, pl.ds(2 * t, 2), :, lanes]
            one = paths[0, pl.ds(2 * t, 2), :, at]
            two = paths[1, pl.ds(2 * t, 2), :, at]
            d_values = d[0] * zero + d[1] * one + d[2] * two
            store_cat(cat_b, 128 + base, 192, at, d_values.reshape(16, LANES))
            store_cat(cat_b, base, 192, at, grad_lat[pl.ds(2 * t, 2), :, at].reshape(16, LANES))
            q = [d[l] * values for l in range(3)]
            for r in range(9):
                level = 0 if r == 0 else (1 if r < 4 else 2)
                term = q[0] if r == 0 else q[level] * harm[r - 1, :, at]
                sums[r][part] = term if sums[r][part] is None else sums[r][part] + term
        found = []
        for r in range(9):
            main, last = sum_slots(sums[r][0].reshape(16, LANES), sums[r][1].reshape(16, LANES))
            found.append((main.reshape(2, 8, LANES), last.reshape(2, 8, LANES)))
        for b, at in enumerate(blocks):
            part = 0 if b < 8 else 1
            lanes = slice(part * LANES, (part + 1) * LANES)
            raw = mixed[pl.ds(8 + 2 * t, 2), :, at]
            envelope = env_live[:, at]
            weight = raw * envelope
            values = mixed[pl.ds(16 + 2 * t, 2), :, at]
            q = [None] + [grad_lat[pl.ds(8 + 8 * l + 2 * t, 2), :, at] * values for l in (1, 2)]
            d_weight = found[0][part]
            for r in range(1, 9):
                g = found[r][part]
                d_weight = d_weight + harm[r - 1, :, at] * g
                level = 1 if r < 4 else 2
                term = q[level] * environment[r, pl.ds(2 * t, 2), :, lanes] + weight * g
                grad_harm[r - 1, :, at] += term[0] + term[1]
            slack = d_weight * raw
            grad_env[:, at] += slack[0] + slack[1]
            store_cat(cat_b, 64 + base, 192, at, (d_weight * envelope).reshape(16, LANES))
        return carry

    lax.fori_loop(0, 4, backward_tile, 0)
    pre[...] = jnp.dot(w3_t_ref[...], cat_b[0:576], preferred_element_type=F32).reshape(16, 8, EDGES)

    def first_back(c, carry):
        back = pre[pl.ds(2 * c, 2)] * slope[pl.ds(2 * c, 2)]
        store_cat(cat_a, 16 * c, 128, slice(None), back.reshape(16, EDGES))
        return carry

    lax.fori_loop(0, 8, first_back, 0)
    d_radial = jnp.dot(win_t_ref[...], cat_a[...], preferred_element_type=F32)[:8]

    x, y, z = harm[0], harm[1], harm[2]
    scaled = x * x + y * y + z * z
    live = jnp.broadcast_to(live_ref[...], (8, EDGES))
    d_scaled = d_radial * (orders * radial_sin) * (-math.pi) + (grad_env[...] + energy[...]) * (
        -2.0 * (1.0 - scaled) * live
    )
    g = [grad_harm[r] for r in range(8)]
    twice = 2.0 * d_scaled
    d_x = g[0] + ROOT3 * (y * g[3] + z * g[5] + x * g[6]) - x * g[7] + twice * x
    d_y = g[1] + ROOT3 * (x * g[3] + z * g[4] - y * g[6]) - y * g[7] + twice * y
    d_z = g[2] + ROOT3 * (y * g[4] + x * g[5]) + 2.0 * z * g[7] + twice * z
    e = energy[...] * env_live[...]
    rows = [jnp.sum(v, axis=0, keepdims=True) for v in (d_x * 0.2, d_y * 0.2, d_z * 0.2, e)]
    grads = jnp.concatenate(rows + [jnp.zeros((4, EDGES), F32)], axis=0)

    def over_blocks(v):
        total = v[:, blocks[0]]
        for b in range(1, 8):
            total = total + v[:, blocks[b]]
        return total

    main, last = sum_slots(over_blocks(grads), grads[:, blocks[8]])
    atoms = jnp.concatenate([main[:, :MAIN], last[:, : ATOMS - MAIN]], axis=1)
    local_ref[...] = atoms
    energy_ref[...] = atoms[3:4]

    extended_grad = exact_dot_nt(grads, hot[...])
    ext_ref[...] = extended_grad[:4]
    lane = lax.broadcasted_iota(jnp.int32, (8, LANES), 1)
    row = lax.broadcasted_iota(jnp.int32, (8, LANES), 0)
    virial = jnp.zeros((8, LANES), F32)
    for a, comp in enumerate((x, y, z)):
        product = comp * grads
        total = jnp.sum(over_blocks(product) + product[:, blocks[8]], axis=1, keepdims=True)
        virial = jnp.where((lane == row + 3 * a) & (row < 3), total * 5.0, virial)
    virial = jnp.sum(virial, axis=0, keepdims=True)
    message = jnp.concatenate([extended_grad[:3, :LANES], virial], axis=0)
    msg_ref[...] = jnp.broadcast_to(message[None], (COUNT * COUNT, 4, LANES))


def middle_kernel(recv_ref, ext_ref, back_ref, msg_ref, keep_ref):
    columns = [recv_ref[neighbour(n)] for n in range(8)] + [ext_ref[...]]
    arrived = pad_rows(jnp.concatenate(columns, axis=1))
    sums = exact_dot(arrived, back_ref[...])
    total = jnp.sum(recv_ref[...], axis=0)
    message = jnp.concatenate([sums[:3, :LANES], total[3:4]], axis=0)
    msg_ref[...] = jnp.broadcast_to(message[None], (COUNT, 4, LANES))
    keep_ref[...] = sums[:, LANES:]


def last_kernel(recv_ref, keep_ref, local_ref, hot_ref, force_ref, virial_ref):
    gz = lax.axis_index("gz")
    above = pad_rows(recv_ref[lax.rem(gz + 1, COUNT)])
    below = pad_rows(recv_ref[lax.rem(gz + (COUNT - 1), COUNT)])
    lane = lax.broadcasted_iota(jnp.int32, (8, LANES), 1)
    row = lax.broadcasted_iota(jnp.int32, (8, LANES), 0)
    sites = keep_ref[...] + jnp.where(lane < 64, pltpu.roll(below, 64, 1), pltpu.roll(above, 64, 1))
    atoms = exact_dot_nt(sites, hot_ref[...])
    force = local_ref[...] - atoms
    for comp in range(3):
        force_ref[comp] = force[comp : comp + 1]
    total = jnp.broadcast_to(jnp.sum(recv_ref[...], axis=0)[3:4], (8, LANES))
    normalizer = -1.0 / math.sqrt(EDGES * COUNT * COUNT * COUNT)
    virial = jnp.zeros((8, LANES), F32)
    for b in range(3):
        entry = jnp.sum(jnp.where(lane == 3 * row + b, total, 0.0), axis=1, keepdims=True)
        virial = jnp.where(lane == b, entry * normalizer, virial)
    virial_ref[...] = virial[:3, :3]


def shape(*dims, dtype=F32):
    return jax.ShapeDtypeStruct(dims, dtype)


def in_hbm(*arrays):
    return [pltpu.with_memory_space_constraint(x, pltpu.HBM) for x in arrays]


def params():
    return pltpu.CompilerParams(vmem_limit_bytes=48 * 1024 * 1024)


def body(
    positions,
    species,
    site_atom,
    edge_center,
    edge_other,
    edge_count,
    w_in,
    w_two,
    w_env,
    w_value,
    w_latent,
    w_out,
    readout,
):
    half = (4, LANES)
    hbm = pl.BlockSpec(memory_space=pltpu.HBM)
    smem = pl.BlockSpec(memory_space=pltpu.SMEM)
    columns_first = jnp.transpose(positions, (1, 0, 2))
    own, down, up, hot = pl.pallas_call(
        send_kernel,
        in_specs=[hbm] * 3,
        out_shape=(shape(*half), shape(*half), shape(*half), shape(ATOMS, LANES, dtype=BF16)),
        scratch_shapes=[
            pltpu.VMEM((3, 1, ATOMS), F32),
            pltpu.VMEM((1, ATOMS), jnp.int32),
            pltpu.VMEM((1, ATOMS), jnp.int32),
            pltpu.SemaphoreType.DMA((3,)),
        ],
        compiler_params=params(),
        name="sites",
    )(*in_hbm(columns_first, species, site_atom))
    ahead = [(i, (i + 1) % COUNT) for i in range(COUNT)]
    behind = [(target, source) for source, target in ahead]
    below = lax.ppermute(up, "gz", ahead)
    above = lax.ppermute(down, "gz", behind)

    inputs = (
        edge_center,
        edge_other,
        columns_first,
        species,
        w_in.T,
        w_two,
        w_env,
        w_value,
        w_latent,
        w_out,
        readout.reshape(1, 64),
    )
    routes = (jnp.asarray(FORWARD, BF16), jnp.asarray(BACK, BF16))
    prepared = pl.pallas_call(
        prepare_kernel,
        in_specs=[smem] + [hbm] * (len(inputs) + 2),
        out_shape=(
            shape(1, EDGES, dtype=jnp.int32),
            shape(1, EDGES),
            shape(8, 256),
            shape(8, 256),
            shape(128, 48, dtype=BF16),
            shape(192, 384, dtype=BF16),
            shape(128, 768, dtype=BF16),
            shape(256, 384, dtype=BF16),
            shape(128, 576, dtype=BF16),
            shape(16, 384, dtype=BF16),
            shape(128, LANES),
            shape(10 * LANES, 256, dtype=BF16),
            shape(10 * LANES, 256, dtype=BF16),
        ),
        scratch_shapes=[pltpu.VMEM(x.shape, x.dtype) for x in inputs] + [pltpu.SemaphoreType.DMA((len(inputs) + 2,))],
        compiler_params=params(),
        cost_estimate=pl.CostEstimate(flops=10_000_000, bytes_accessed=2_000_000, transcendentals=0),
        name="slots_and_weights",
    )(edge_count, *in_hbm(*inputs, *routes))

    planes = (COUNT * COUNT, 4, LANES)
    column, outer = pl.pallas_call(
        column_kernel,
        out_shape=(shape(*planes), shape(*half)),
        compiler_params=params(),
        name="column",
    )(down, up, below, above, prepared[3])
    arrived = lax.all_to_all(column, ("gx", "gy"), 0, 0)

    message, extended_grad, local_grad, site_energy = pl.pallas_call(
        main_kernel,
        out_shape=(shape(*planes), shape(4, 256), shape(8, ATOMS), shape(1, ATOMS)),
        scratch_shapes=[
            pltpu.VMEM((256, EDGES), BF16),
            pltpu.VMEM((8, 8, EDGES), F32),
            pltpu.VMEM((8, EDGES), F32),
            pltpu.VMEM((16, 8, EDGES), F32),
            pltpu.VMEM((16, 8, EDGES), F32),
            pltpu.VMEM((384, EDGES), BF16),
            pltpu.VMEM((768, EDGES), BF16),
            pltpu.VMEM((24, 8, EDGES), F32),
            pltpu.VMEM((2, 8, 8, EDGES), F32),
            pltpu.VMEM((9, 8, 8, 256), F32),
            pltpu.VMEM((32, 8, EDGES), F32),
            pltpu.VMEM((8, 8, EDGES), F32),
            pltpu.VMEM((8, EDGES), F32),
            pltpu.VMEM((8, EDGES), F32),
        ],
        compiler_params=params(),
        name="edges",
    )(arrived, outer, own, *prepared[:12])
    returned = lax.all_to_all(message, ("gx", "gy"), 0, 0)
    layers, keep = pl.pallas_call(
        middle_kernel,
        out_shape=(shape(COUNT, 4, LANES), shape(8, LANES)),
        compiler_params=params(),
        name="columns_back",
    )(returned, extended_grad, prepared[12])
    closing = lax.all_to_all(layers, "gz", 0, 0)
    forces, virial = pl.pallas_call(
        last_kernel,
        out_shape=(shape(3, 1, ATOMS), shape(3, 3)),
        compiler_params=params(),
        name="forces",
    )(closing, keep, local_grad, hot)
    return jnp.transpose(forces, (1, 0, 2)), site_energy, virial


def solution(mesh):
    by_domain = ("gx", "gy", "gz")
    placed = (
        P(by_domain, None, None),
        P(by_domain, None),
        P(by_domain, None),
        P(by_domain, None),
        P(by_domain, None),
        P(by_domain),
    ) + (P(),) * 7
    return jax.shard_map(
        body,
        mesh=mesh,
        in_specs=placed,
        out_specs=(P(by_domain, None, None), P(by_domain, None), P()),
        check_vma=False,
    )
```

time: 300 us -> 74.3 us (0.25)
  other arithmetic: 65.2 us -> 0 us
  local copies, waits for them, and re-layouts: 59.1 us -> 0 us
  blocking collectives: 99.2 us -> 46.1 us
  starting transfers between devices: 56.4 us -> 13.4 us
  matrix products: 15.2 us -> 0 us
  Pallas kernels: 0 us -> 12.2 us
    psum x1 -> x0, blocking collectives: 99.2 us -> none  [body(): virial = lax.psum(virial_part, ('gx', 'gy', 'gz')) * normalizer]
    scatter-add x6 -> x0, other arithmetic: 51.2 us -> none  [the longest x1 11.6 us: domain_energy(): jnp.take(environment, center, axis=1).reshape(9, channels, edge_total)]
    all_to_all x0 -> x3, blocking collectives: none -> 46.1 us  [the longest x1 22.1 us: body(): arrived = lax.all_to_all(column, ('gx', 'gy'), 0, 0)]
    gather x14 -> x0, local copies, waits for them, and re-layouts: 44.4 us -> none  [the longest x2 8.19 us: domain_energy(): jnp.zeros((9 * channels, atom_count), jnp.float32).at[:, center]]
    ppermute x12 -> x2, starting transfers between devices: 56.4 us -> 13.4 us  [the longest x1 11.5 us: body(): above = lax.ppermute(down, 'gz', behind)]
    dot_general x15 -> x0, matrix products: 15.2 us -> none  [matmul(): jnp.dot(left, right, precision=highest, preferred_element_type=jnp.float32)]
    pallas_call x0 -> x6, Pallas kernels: none -> 12.2 us  [the longest x1 7.64 us: body(): pl.pallas_call(main_kernel, out_shape=(shape(*planes), shape(4, 256), sha...]
    unnamed x100 -> x0, local copies, waits for them, and re-layouts: 6.13 us -> none
  transfers between devices with their start and end apart: 12 -> 2, of which waited for: 2 -> 1; matrix products, arithmetic and copies ran while one was open for 13% -> 0% of each run, Pallas kernels for 0% -> 3%
where the time goes in v1:
time: 74.3 us; the launch traced here: 73.5 us
  blocking collectives  46.1 us (62%)
  starting transfers between devices  13.4 us (18%)
  Pallas kernels  12.2 us (16%)
  between operations  1.33 us (2%)
    all_to_all x1, blocking collectives, body(): arrived = lax.all_to_all(column, ('gx', 'gy'), 0, 0)  22.1 us
    all_to_all x1, blocking collectives, body(): returned = lax.all_to_all(message, ('gx', 'gy'), 0, 0)  14.9 us
    ppermute x1, starting transfers between devices, body(): above = lax.ppermute(down, 'gz', behind)  11.5 us
    all_to_all x1, blocking collectives, body(): closing = lax.all_to_all(layers, 'gz', 0, 0)  9.02 us
    pallas_call x1, Pallas kernels, body(): pl.pallas_call(main_kernel, out_shape=(shape(*planes), shape(4, 256), sha...  7.64 us
    pallas_call x1, Pallas kernels, body(): pl.pallas_call(prepare_kernel, in_specs=[smem] + [hbm] * (len(inputs) + 2...  2.46 us
    ppermute x1, starting transfers between devices, body(): below = lax.ppermute(up, 'gz', ahead)  1.92 us
  transfers between devices with their start and end apart: 2, of which 1 were waited for; matrix products, arithmetic and copies ran while one was open for 0% of the time, Pallas kernels for 3%

profile of v1, /device:TPU:1, one launch (start us, length us, event | category | flops | bytes accessed | tf_op | source)
XLA Modules:
  0.0 73.5 jit_solution(1087329931726834325)
XLA Ops:
  0.6 1.0 %sites.1 = (f32[4,128]{1,0:T(4,128)S(1)}, f32[4,128]{1,0:T(4,128)S(1)}, f32[4,128]{1,0:T(4,128)S(1)}, bf16[72,128]{1,0:T(8,128)(2,1)S(1)}) custom-call(f32[3,1,72]{2,1,0:T(1,128)} %bitcast.5, s32[1,72]{1,0:T(1,128)} %refs_3_.1, s32[1,72]{1,0:T(1,128)} %site_hbm.1), custom_call_target="tpu_custom_call" | custom-call | tf_op jit(solution)/shard_map/sites/pallas_call | solution.py:625
  1.6 11.5 %collective-permute-start.1 = (f32[4,128]{1,0:T(4,128)S(1)}, f32[4,128]{1,0:T(4,128)S(1)}, u32[]{:S(2)}, u32[]{:S(2)}) collective-permute-start(f32[4,128]{1,0:T(4,128)S(1)} %get-tuple-element.30.down_ref), channel_id=1, source_target_pairs={{1,0},{2,1},{3,2},{4,3},{5,4},{6,5},{7,6},{0,7},{9,8},{10,9},{11,1... | collective-permute-start | bytes 6152 | tf_op jit(solution)/shard_map/ppermute | solution.py:641
  13.2 1.9 %collective-permute-start = (f32[4,128]{1,0:T(4,128)S(1)}, f32[4,128]{1,0:T(4,128)S(1)}, u32[]{:S(2)}, u32[]{:S(2)}) collective-permute-start(f32[4,128]{1,0:T(4,128)S(1)} %get-tuple-element.31.up_ref), channel_id=1, source_target_pairs={{0,1},{1,2},{2,3},{3,4},{4,5},{5,6},{6,7},{7,0},{8,9},{9,10},{10,1... | collective-permute-start | bytes 6152 | tf_op jit(solution)/shard_map/ppermute | solution.py:640
  15.7 2.5 %slots_and_weights.1 = (s32[1,1152]{1,0:T(1,128)S(1)}, f32[1,1152]{1,0:T(1,128)S(1)}, f32[8,256]{1,0:T(8,128)S(1)}, f32[8,256]{1,0:T(8,128)S(1)}, bf16[128,48]{1...) custom-call(s32[1]{0:T(128)S(6)} %copy.18.count_ref, ...), custom_call_target="tpu_custom_call" | custom-call | flops 10000000 | bytes 2000000 | tf_op jit(solution)/shard_map/slots_and_weights/pallas_call | solution.py:657
  18.2 0.0 collective-permute-done.1.above_ref
  18.2 0.5 collective-permute-done.below_ref
  18.7 0.1 column.1
  18.8 22.1 %all_to_all.15.recv_ref = f32[64,4,128]{2,1,0:T(4,128)S(1)} all-to-all(f32[64,4,128]{2,1,0:T(4,128)S(1)} %get-tuple-element.33), channel_id=1, replica_groups=mesh['gx'=8,'gy'=8,'gz'=8] {'gx','gy'}, dimensions={0} | all-to-all | bytes 262144 | tf_op jit(solution)/shard_map/all_to_all | solution.py:688
  40.9 7.6 %edges.1 = (f32[64,4,128]{2,1,0:T(4,128)S(1)}, f32[4,256]{1,0:T(4,128)S(1)}, f32[8,72]{1,0:T(8,128)S(1)}, f32[1,72]{1,0:T(1,128)}) custom-call(f32[64,4,128]{2,1,0:T(4,128)S(1)} %all_to_all.15.recv_ref, f32[4,128]{1,0:T(4,128)S(1)} %get-tuple-element.34.outer_ref, f32[4,128]{1,0:T(4,128)S(1)} %get-tuple-element.35.inner_ref, ...), custom_call_target="tpu_custom_call" | custom-call | tf_op jit(solution)/shard_map/edges/pallas_call | solution.py:690
  48.5 14.9 %all_to_all.16.recv_ref = f32[64,4,128]{2,1,0:T(4,128)S(1)} all-to-all(f32[64,4,128]{2,1,0:T(4,128)S(1)} %get-tuple-element.47), channel_id=1, replica_groups=mesh['gx'=8,'gy'=8,'gz'=8] {'gx','gy'}, dimensions={0} | all-to-all | bytes 262144 | tf_op jit(solution)/shard_map/all_to_all | solution.py:712
  63.5 0.2 columns_back.1
  63.7 9.0 %all_to_all.17.recv_ref = f32[8,4,128]{2,1,0:T(4,128)S(1)} all-to-all(f32[8,4,128]{2,1,0:T(4,128)S(1)} %get-tuple-element.50), channel_id=1, replica_groups=mesh['gx'=8,'gy'=8,'gz'=8] {'gz'}, dimensions={0} | all-to-all | bytes 32768 | tf_op jit(solution)/shard_map/all_to_all | solution.py:719
  72.7 0.8 %forces.1 = (f32[3,1,72]{2,1,0:T(1,128)}, f32[3,3]{1,0:T(4,128)}) custom-call(f32[8,4,128]{2,1,0:T(4,128)S(1)} %all_to_all.17.recv_ref, f32[8,128]{1,0:T(8,128)S(1)} %get-tuple-element.51.keep_ref, f32[8,72]{1,0:T(8,128)S(1)} %get-tuple-element.52.local_ref, bf16[72,128]{1,0:T(8,128)(2,1)S(1)} %get-tuple-element.53.hot_ref), custom_call_target="tpu_custom_call" | custom-call | tf_op jit(solution)/shard_map/forces/pallas_call | solution.py:720
Async XLA Ops:
  1.6 16.5 %collective-permute-start.1 = (f32[4,128]{1,0:T(4,128)S(1)}, f32[4,128]{1,0:T(4,128)S(1)}, u32[]{:S(2)}, u32[]{:S(2)}) collective-permute-start(f32[4,128]{1,0:T(4,128)S(1)} %get-tuple-element.30.down_ref), channel_id=1, source_target_pairs={{1,0},{2,1},{3,2},{4,3},{5,4},{6,5},{7,6},{0,7},{9,8},{10,9},{11,1... | collective-permute-start | bytes 6152 | tf_op jit(solution)/shard_map/ppermute | solution.py:641
  13.2 5.5 %collective-permute-start = (f32[4,128]{1,0:T(4,128)S(1)}, f32[4,128]{1,0:T(4,128)S(1)}, u32[]{:S(2)}, u32[]{:S(2)}) collective-permute-start(f32[4,128]{1,0:T(4,128)S(1)} %get-tuple-element.31.up_ref), channel_id=1, source_target_pairs={{0,1},{1,2},{2,3},{3,4},{4,5},{5,6},{6,7},{7,0},{8,9},{9,10},{10,1... | collective-permute-start | bytes 6152 | tf_op jit(solution)/shard_map/ppermute | solution.py:640

commit v2 on v1

--- a/solution.py
+++ b/solution.py
@@ -48,39 +48,52 @@
     return 112 + k * 36 + (i - 1) * 6 + (j - 1)
 
 
+SITE_RANGE = {1: [5], -1: [0], 0: list(range(6))}
+CELL_RANGE = {1: [7], -1: [0], 0: list(range(1, 7))}
+
+
+def face(ranges, dx, dy):
+    return list(enumerate((a, b) for a in ranges[dx] for b in ranges[dy]))
+
+
 def tables():
-    forward = np.zeros((10 * LANES, 256), np.float32)
+    send_sites = np.full((8, 4, 4, 8), -1, np.int32)
+    send_cells = np.full((8, 4, 4, 8), -1, np.int32)
+    source = np.full((256,), -1, np.int32)
+    target = np.full((10 * LANES,), -1, np.int32)
+    places = {0: 0, 3: 64, 1: LANES, 2: LANES + 64}
+    landing = target[: 8 * LANES].reshape(8, 4, 4, 8)
     for n, (dx, dy) in enumerate(STEPS):
-        for m, (x, y) in enumerate(RIM_SITES):
-            i = {0: x + 1, 1: 7 if x == 0 else None, -1: 0 if x == 5 else None}[dx]
-            j = {0: y + 1, 1: 7 if y == 0 else None, -1: 0 if y == 5 else None}[dy]
-            if i is None or j is None:
-                continue
+        for at, site in face(SITE_RANGE, dx, dy):
             for k in range(4):
-                forward[n * LANES + k * 32 + m, cell_number(i, j, k)] = 1.0
-    for x in range(CELLS):
-        for y in range(CELLS):
-            for k, at in ((0, 0), (3, 64), (1, LANES), (2, LANES + 64)):
-                forward[8 * LANES + at + x * 6 + y, cell_number(x + 1, y + 1, k)] = 1.0
-    back = np.zeros((10 * LANES, 256), np.float32)
-    places = {0: 0, 3: 64, 1: LANES, 2: LANES + 64}
-    for n, (dx, dy) in enumerate(STEPS):
-        for i in range(8):
-            for j in range(8):
-                if not (i in (0, 7) or j in (0, 7)):
-                    continue
-                x, y = dx * 6 + i - 1, dy * 6 + j - 1
-                if 0 <= x < 6 and 0 <= y < 6:
-                    for k in range(4):
-                        back[n * LANES + cell_number(i, j, k), places[k] + x * 6 + y] = 1.0
+                send_sites[n, :, k, at] = k * 32 + RIM_SITES.index(site)
+        for at, (i, j) in face(CELL_RANGE, dx, dy):
+            for k in range(4):
+                send_cells[n, :3, k, at] = cell_number(i, j, k)
+        for at, (x, y) in face(SITE_RANGE, -dx, -dy):
+            i = {1: 7, -1: 0, 0: x + 1}[dx]
+            j = {1: 7, -1: 0, 0: y + 1}[dy]
+            for k in range(4):
+                source[cell_number(i, j, k)] = n * LANES + k * 8 + at
+        for at, (i, j) in face(CELL_RANGE, -dx, -dy):
+            x = {1: 5, -1: 0, 0: i - 1}[dx]
+            y = {1: 5, -1: 0, 0: j - 1}[dy]
+            for k in range(4):
+                landing[n, :3, k, at] = places[k] + x * 6 + y
     for x in range(CELLS):
         for y in range(CELLS):
             for k in range(4):
-                back[8 * LANES + cell_number(x + 1, y + 1, k), places[k] + x * 6 + y] = 1.0
-    return forward, back
-
-
-FORWARD, BACK = tables()
+                own = cell_number(x + 1, y + 1, k)
+                source[own] = 8 * LANES + places[k] + x * 6 + y
+                target[8 * LANES + own] = places[k] + x * 6 + y
+    row = np.arange(10 * LANES)[:, None]
+    forward = np.where(row < 8 * LANES, row & ~96, row) == source
+    back = target[:, None] == np.arange(256)
+    lane = np.arange(LANES)[:, None]
+    return forward, back, lane == send_sites.reshape(-1), lane == send_cells.reshape(-1)
+
+
+TABLES = tables()
 
 
 def parts_of(x, count):
@@ -121,11 +134,15 @@
     return jnp.where(mask, 1.0, 0.0).astype(BF16)
 
 
-def fetch(sources, buffers, sems):
+def start_fetch(sources, buffers, sems):
     copies = [pltpu.make_async_copy(src, dst, sems.at[n]) for n, (src, dst) in enumerate(zip(sources, buffers))]
     for copy in copies:
         copy.start()
-    for copy in copies:
+    return copies
+
+
+def fetch(sources, buffers, sems):
+    for copy in start_fetch(sources, buffers, sems):
         copy.wait()
 
 
@@ -149,33 +166,54 @@
     return 2 * jnp.where((part > 0) & second, rim, whole) + layer
 
 
-def send_kernel(pos_hbm, kind_hbm, site_hbm, own_ref, down_ref, up_ref, hot_ref, pos_ref, kind_ref, site_ref, sems):
+def send_kernel(pos_hbm, kind_hbm, site_hbm, both_ref, down_ref, up_ref, hot_ref, pos_ref, kind_ref, site_ref, sems):
     fetch((pos_hbm, kind_hbm, site_hbm), (pos_ref, kind_ref, site_ref), sems)
     rows = atom_rows(pos_ref, kind_ref)
     hot = as_hot(iota((ATOMS, ATOMS), 0) == site_ref[...])
     pick = as_hot(iota((ATOMS, 3 * LANES), 0) == lane_sites()[0:1])
     placed = jnp.dot(hot, pick, preferred_element_type=F32).astype(BF16)
     out = exact_dot(rows, placed)
-    own_ref[...] = out[:4, 0:LANES]
+    both_ref[...] = out[:4, 0:LANES]
     down_ref[...] = out[:4, LANES : 2 * LANES]
     up_ref[...] = out[:4, 2 * LANES : 3 * LANES]
     hot_ref[...] = placed[:, 0:LANES]
 
 
-def column_kernel(down_ref, up_ref, below_ref, above_ref, tie_ref, msg_ref, outer_ref):
-    lane = lax.broadcasted_iota(jnp.int32, (8, LANES), 1)
+def by_component(row):
+    lane, comp = iota((8, LANES), 1), iota((8, LANES), 0)
+    return jnp.where((lane >> 5) == comp, jnp.broadcast_to(row, (8, LANES)), 0.0)
+
+
+def to_rows(x, table):
+    out = exact_dot(x, table)
+    keep = ((iota(out.shape, 1) >> 5) & 3) == iota(out.shape, 0)
+    return jnp.sum(jnp.where(keep, out, 0.0), axis=0, keepdims=True)
+
+
+def neighbour(n):
+    dx, dy = STEPS[n]
+    gx = lax.axis_index("gx")
+    gy = lax.axis_index("gy")
+    return lax.rem(gx + (dx + COUNT), COUNT) * COUNT + lax.rem(gy + (dy + COUNT), COUNT)
+
+
+def column_kernel(down_ref, up_ref, below_ref, above_ref, table_ref, msg_ref, outer_ref):
+    lane = iota((8, LANES), 1)
 
     def rim(x, at):
         return pltpu.roll(x, (at - 64) % LANES, 1)
 
     below, above, low, high = (pad_rows(ref[...]) for ref in (below_ref, above_ref, down_ref, up_ref))
-    msg = jnp.where(
+    column = jnp.where(
         lane < 32,
         rim(below, 0),
         jnp.where(lane < 64, rim(low, 32), jnp.where(lane < 96, rim(high, 64), rim(above, 96))),
     )
     outer_ref[...] = jnp.where(lane < 64, below, pltpu.roll(above, 64, 1))[:4]
-    msg_ref[...] = jnp.broadcast_to(msg[:4][None], (COUNT * COUNT, 4, LANES))
+    rows = to_rows(column, table_ref[...])
+    msg_ref[...] = jnp.zeros_like(msg_ref)
+    for n in range(8):
+        msg_ref[pl.ds(neighbour(n), 1), :] = rows[:, n * LANES : (n + 1) * LANES]
 
 
 def cat_of(w):
@@ -216,16 +254,23 @@
 
 
 def prepare_kernel(count_ref, *refs):
-    sources, outputs, buffers, sems = refs[:13], refs[13:26], refs[26:37], refs[37]
-    cell_ref, live_ref, own_ref, shift_ref = outputs[:4]
-    win_ref, w3_ref, wlat_ref, wlat_t_ref, w3_t_ref, win_t_ref, read_ref = outputs[4:11]
-    fetch(sources, buffers + outputs[11:], sems)
-    center_ref, other_ref, pos_ref, kind_ref, w_in_ref, w_two_ref, w_env_ref = buffers[:7]
-    w_value_ref, w_latent_ref, w_out_ref, readout_ref = buffers[7:]
+    sources, outputs, buffers, sems = refs[:15], refs[15:30], refs[30:41], refs[41]
+    copies = start_fetch(sources, buffers + outputs[11:], sems)
+    make_slots(count_ref, copies[:4], buffers[:4], outputs[:4])
+    make_weights(copies[4:11], buffers[4:], outputs[4:11])
+    for copy in copies[11:]:
+        copy.wait()
+
+
+def make_slots(count_ref, copies, buffers, outputs):
+    center_ref, other_ref, pos_ref, kind_ref = buffers
+    cell_ref, live_ref, own_ref, shift_ref = outputs
     shift_ref[...] = cell_shifts()
     before = as_hot((iota((LANES, 256), 0) < iota((LANES, 256), 1)) | (iota((LANES, 256), 1) >= LANES))
     lane = iota((ATOMS, 256), 1)
     spread = as_hot(iota((ATOMS, 256), 0) == jnp.where(lane < LANES, lane & 63, MAIN + (lane & 7)))
+    for copy in copies:
+        copy.wait()
     center = center_ref[...]
     other = other_ref[...]
     atom = lax.broadcasted_iota(jnp.int32, (ATOMS, EDGES), 0)
@@ -261,6 +306,12 @@
         live_ref[:, at] = placed[16 + b : 17 + b]
     own_ref[...] = exact_dot(atom_rows(pos_ref, kind_ref), spread)
 
+
+def make_weights(copies, buffers, outputs):
+    win_ref, w3_ref, wlat_ref, wlat_t_ref, w3_t_ref, win_t_ref, read_ref = outputs
+    for copy in copies:
+        copy.wait()
+    w_in_ref, w_two_ref, w_env_ref, w_value_ref, w_latent_ref, w_out_ref, readout_ref = buffers
     w_in_t = w_in_ref[...]
     win_ref[...] = cat_of(w_in_t.T)
     w_two = w_two_ref[...]
@@ -313,16 +364,14 @@
 def store_cat(ref, row, depth, at, x):
     high = x.astype(BF16)
     low = (x - high.astype(F32)).astype(BF16)
-    ref[pl.ds(pl.multiple_of(row, 16), 16), at] = high
-    ref[pl.ds(pl.multiple_of(depth + row, 16), 16), at] = low
-    ref[pl.ds(pl.multiple_of(2 * depth + row, 16), 16), at] = high
-
-
-def neighbour(n):
-    dx, dy = STEPS[n]
-    gx = lax.axis_index("gx")
-    gy = lax.axis_index("gy")
-    return lax.rem(gx + (dx + COUNT), COUNT) * COUNT + lax.rem(gy + (dy + COUNT), COUNT)
+    ref[pl.ds(row, 16), at] = high
+    ref[pl.ds(depth + row, 16), at] = low
+    ref[pl.ds(2 * depth + row, 16), at] = high
+
+
+def repeat(count, step):
+    for n in range(count):
+        step(n, 0)
 
 
 def main_kernel(
@@ -341,10 +390,10 @@
     win_t_ref,
     read_ref,
     forward_ref,
+    cells_ref,
     msg_ref,
     ext_ref,
     local_ref,
-    energy_ref,
     hot,
     harm,
     env_live,
@@ -362,8 +411,9 @@
 ):
     blocks = [slice(b * LANES, (b + 1) * LANES) for b in range(BLOCKS)]
 
-    columns = [recv_ref[neighbour(n)] for n in range(8)] + [outer_ref[...], inner_ref[...]]
-    arrived = pad_rows(jnp.concatenate(columns, axis=1))
+    columns = [by_component(recv_ref[pl.ds(neighbour(n), 1), :]) for n in range(8)]
+    columns += [pad_rows(outer_ref[...]), pad_rows(inner_ref[...])]
+    arrived = jnp.concatenate(columns, axis=1)
     extended = exact_dot(arrived, forward_ref[...]) + shift_ref[...]
     cells = lax.broadcasted_iota(jnp.int32, (256, EDGES), 0)
     hot[...] = jnp.where(cells == cell_ref[...], 1.0, 0.0).astype(BF16)
@@ -412,7 +462,7 @@
         store_cat(cat_a, 16 * c, 128, slice(None), out.reshape(16, EDGES))
         return carry
 
-    lax.fori_loop(0, 8, first_layer, 0)
+    repeat(8, first_layer)
     mixed[...] = jnp.dot(w3_ref[...], cat_a[0:384], preferred_element_type=F32).reshape(24, 8, EDGES)
 
     def forward_tile(t, carry):
@@ -446,7 +496,7 @@
             store_cat(cat_b, 192 + base, 256, at, (two * values).reshape(16, LANES))
         return carry
 
-    lax.fori_loop(0, 4, forward_tile, 0)
+    repeat(4, forward_tile)
     pre[...] = jnp.dot(wlat_ref[...], cat_b[...], preferred_element_type=F32).reshape(16, 8, EDGES)
     energy[...] = jnp.zeros((8, EDGES), F32)
 
@@ -454,7 +504,7 @@
         v = pre[pl.ds(2 * c, 2)]
         gate = 1.0 / (1.0 + jnp.exp(-v))
         out = v * gate
-        weights = read_ref[pl.ds(pl.multiple_of(16 * c, 16), 16), :].reshape(2, 8, LANES)
+        weights = read_ref[pl.ds(16 * c, 16), :].reshape(2, 8, LANES)
         weights = jnp.concatenate([weights] * BLOCKS, axis=2)
         product = weights * out
         energy[...] += product[0] + product[1]
@@ -462,7 +512,7 @@
         store_cat(cat_a, 16 * c, 128, slice(None), back.reshape(16, EDGES))
         return carry
 
-    lax.fori_loop(0, 8, second_layer, 0)
+    repeat(8, second_layer)
     grad_lat[...] = jnp.dot(wlat_t_ref[...], cat_a[...], preferred_element_type=F32).reshape(32, 8, EDGES)
     grad_harm[...] = jnp.zeros((8, 8, EDGES), F32)
     grad_env[...] = jnp.zeros((8, EDGES), F32)
@@ -510,7 +560,7 @@
             store_cat(cat_b, 64 + base, 192, at, (d_weight * envelope).reshape(16, LANES))
         return carry
 
-    lax.fori_loop(0, 4, backward_tile, 0)
+    repeat(4, backward_tile)
     pre[...] = jnp.dot(w3_t_ref[...], cat_b[0:576], preferred_element_type=F32).reshape(16, 8, EDGES)
 
     def first_back(c, carry):
@@ -518,7 +568,7 @@
         store_cat(cat_a, 16 * c, 128, slice(None), back.reshape(16, EDGES))
         return carry
 
-    lax.fori_loop(0, 8, first_back, 0)
+    repeat(8, first_back)
     d_radial = jnp.dot(win_t_ref[...], cat_a[...], preferred_element_type=F32)[:8]
 
     x, y, z = harm[0], harm[1], harm[2]
@@ -545,7 +595,6 @@
     main, last = sum_slots(over_blocks(grads), grads[:, blocks[8]])
     atoms = jnp.concatenate([main[:, :MAIN], last[:, : ATOMS - MAIN]], axis=1)
     local_ref[...] = atoms
-    energy_ref[...] = atoms[3:4]
 
     extended_grad = exact_dot_nt(grads, hot[...])
     ext_ref[...] = extended_grad[:4]
@@ -555,23 +604,25 @@
     for a, comp in enumerate((x, y, z)):
         product = comp * grads
         total = jnp.sum(over_blocks(product) + product[:, blocks[8]], axis=1, keepdims=True)
-        virial = jnp.where((lane == row + 3 * a) & (row < 3), total * 5.0, virial)
+        virial = jnp.where((lane == 96 + row + 3 * a) & (row < 3), total * 5.0, virial)
     virial = jnp.sum(virial, axis=0, keepdims=True)
-    message = jnp.concatenate([extended_grad[:3, :LANES], virial], axis=0)
-    msg_ref[...] = jnp.broadcast_to(message[None], (COUNT * COUNT, 4, LANES))
+    rows = to_rows(extended_grad[:, :LANES], cells_ref[...])
+    msg_ref[...] = jnp.broadcast_to(virial, (COUNT * COUNT, LANES))
+    for n in range(8):
+        msg_ref[pl.ds(neighbour(n), 1), :] = rows[:, n * LANES : (n + 1) * LANES] + virial
 
 
 def middle_kernel(recv_ref, ext_ref, back_ref, msg_ref, keep_ref):
-    columns = [recv_ref[neighbour(n)] for n in range(8)] + [ext_ref[...]]
-    arrived = pad_rows(jnp.concatenate(columns, axis=1))
+    columns = [by_component(recv_ref[pl.ds(neighbour(n), 1), :]) for n in range(8)]
+    arrived = jnp.concatenate(columns + [pad_rows(ext_ref[...])], axis=1)
     sums = exact_dot(arrived, back_ref[...])
-    total = jnp.sum(recv_ref[...], axis=0)
-    message = jnp.concatenate([sums[:3, :LANES], total[3:4]], axis=0)
+    total = jnp.sum(recv_ref[...], axis=0, keepdims=True)
+    message = jnp.concatenate([sums[:3, :LANES], total], axis=0)
     msg_ref[...] = jnp.broadcast_to(message[None], (COUNT, 4, LANES))
     keep_ref[...] = sums[:, LANES:]
 
 
-def last_kernel(recv_ref, keep_ref, local_ref, hot_ref, force_ref, virial_ref):
+def last_kernel(recv_ref, keep_ref, local_ref, hot_ref, force_ref, energy_ref, virial_ref):
     gz = lax.axis_index("gz")
     above = pad_rows(recv_ref[lax.rem(gz + 1, COUNT)])
     below = pad_rows(recv_ref[lax.rem(gz + (COUNT - 1), COUNT)])
@@ -579,6 +630,7 @@
     row = lax.broadcasted_iota(jnp.int32, (8, LANES), 0)
     sites = keep_ref[...] + jnp.where(lane < 64, pltpu.roll(below, 64, 1), pltpu.roll(above, 64, 1))
     atoms = exact_dot_nt(sites, hot_ref[...])
+    energy_ref[...] = local_ref[3:4]
     force = local_ref[...] - atoms
     for comp in range(3):
         force_ref[comp] = force[comp : comp + 1]
@@ -586,7 +638,7 @@
     normalizer = -1.0 / math.sqrt(EDGES * COUNT * COUNT * COUNT)
     virial = jnp.zeros((8, LANES), F32)
     for b in range(3):
-        entry = jnp.sum(jnp.where(lane == 3 * row + b, total, 0.0), axis=1, keepdims=True)
+        entry = jnp.sum(jnp.where(lane == 96 + 3 * row + b, total, 0.0), axis=1, keepdims=True)
         virial = jnp.where(lane == b, entry * normalizer, virial)
     virial_ref[...] = virial[:3, :3]
 
@@ -597,6 +649,10 @@
 
 def in_hbm(*arrays):
     return [pltpu.with_memory_space_constraint(x, pltpu.HBM) for x in arrays]
+
+
+def fetched(arrays, more=0):
+    return [pltpu.VMEM(x.shape, x.dtype) for x in arrays] + [pltpu.SemaphoreType.DMA((len(arrays) + more,))]
 
 
 def params():
@@ -620,7 +676,6 @@
 ):
     half = (4, LANES)
     hbm = pl.BlockSpec(memory_space=pltpu.HBM)
-    smem = pl.BlockSpec(memory_space=pltpu.SMEM)
     columns_first = jnp.transpose(positions, (1, 0, 2))
     own, down, up, hot = pl.pallas_call(
         send_kernel,
@@ -653,10 +708,10 @@
         w_out,
         readout.reshape(1, 64),
     )
-    routes = (jnp.asarray(FORWARD, BF16), jnp.asarray(BACK, BF16))
+    routes = [jnp.asarray(table, BF16) for table in TABLES]
     prepared = pl.pallas_call(
         prepare_kernel,
-        in_specs=[smem] + [hbm] * (len(inputs) + 2),
+        in_specs=[pl.BlockSpec(memory_space=pltpu.SMEM)] + [hbm] * (len(inputs) + 4),
         out_shape=(
             shape(1, EDGES, dtype=jnp.int32),
             shape(1, EDGES),
@@ -671,25 +726,27 @@
             shape(128, LANES),
             shape(10 * LANES, 256, dtype=BF16),
             shape(10 * LANES, 256, dtype=BF16),
+            shape(LANES, 8 * LANES, dtype=BF16),
+            shape(LANES, 8 * LANES, dtype=BF16),
         ),
-        scratch_shapes=[pltpu.VMEM(x.shape, x.dtype) for x in inputs] + [pltpu.SemaphoreType.DMA((len(inputs) + 2,))],
+        scratch_shapes=fetched(inputs, 4),
         compiler_params=params(),
         cost_estimate=pl.CostEstimate(flops=10_000_000, bytes_accessed=2_000_000, transcendentals=0),
         name="slots_and_weights",
     )(edge_count, *in_hbm(*inputs, *routes))
 
-    planes = (COUNT * COUNT, 4, LANES)
+    planes = (COUNT * COUNT, LANES)
     column, outer = pl.pallas_call(
         column_kernel,
         out_shape=(shape(*planes), shape(*half)),
         compiler_params=params(),
         name="column",
-    )(down, up, below, above, prepared[3])
+    )(down, up, below, above, prepared[13])
     arrived = lax.all_to_all(column, ("gx", "gy"), 0, 0)
 
-    message, extended_grad, local_grad, site_energy = pl.pallas_call(
+    message, extended_grad, local_grad = pl.pallas_call(
         main_kernel,
-        out_shape=(shape(*planes), shape(4, 256), shape(8, ATOMS), shape(1, ATOMS)),
+        out_shape=(shape(*planes), shape(4, 256), shape(8, ATOMS)),
         scratch_shapes=[
             pltpu.VMEM((256, EDGES), BF16),
             pltpu.VMEM((8, 8, EDGES), F32),
@@ -708,7 +765,7 @@
         ],
         compiler_params=params(),
         name="edges",
-    )(arrived, outer, own, *prepared[:12])
+    )(arrived, outer, own, *prepared[:12], prepared[14])
     returned = lax.all_to_all(message, ("gx", "gy"), 0, 0)
     layers, keep = pl.pallas_call(
         middle_kernel,
@@ -717,9 +774,9 @@
         name="columns_back",
     )(returned, extended_grad, prepared[12])
     closing = lax.all_to_all(layers, "gz", 0, 0)
-    forces, virial = pl.pallas_call(
+    forces, site_energy, virial = pl.pallas_call(
         last_kernel,
-        out_shape=(shape(3, 1, ATOMS), shape(3, 3)),
+        out_shape=(shape(3, 1, ATOMS), shape(1, ATOMS), shape(3, 3)),
         compiler_params=params(),
         name="forces",
     )(closing, keep, local_grad, hot)

time: 74.3 us -> 67.7 us (0.911)
  Pallas kernels: 12.2 us -> 8.29 us
  blocking collectives: 46.1 us -> 43.3 us
    pallas_call x1, Pallas kernels: 7.64 us -> 4.19 us  [body(): pl.pallas_call(main_kernel, out_shape=(shape(*planes), shape(4, 256), sha...]
    all_to_all x1, blocking collectives: 14.9 us -> 13.1 us  [body(): returned = lax.all_to_all(message, ('gx', 'gy'), 0, 0)]
    all_to_all x1, blocking collectives: 22.1 us -> 21.2 us  [body(): arrived = lax.all_to_all(column, ('gx', 'gy'), 0, 0)]
where the time goes in v2:
time: 67.7 us; the launch traced here: 67.4 us
  blocking collectives  43.3 us (64%)
  starting transfers between devices  13.4 us (20%)
  Pallas kernels  8.29 us (12%)
  between operations  1.34 us (2%)
  waiting for transfers between devices  1.06 us (2%)
    all_to_all x1, blocking collectives, body(): arrived = lax.all_to_all(column, ('gx', 'gy'), 0, 0)  21.2 us
    all_to_all x1, blocking collectives, body(): returned = lax.all_to_all(message, ('gx', 'gy'), 0, 0)  13.1 us
    ppermute x1, starting transfers between devices, body(): above = lax.ppermute(down, 'gz', behind)  11.5 us
    all_to_all x1, blocking collectives, body(): closing = lax.all_to_all(layers, 'gz', 0, 0)  9 us
    pallas_call x1, Pallas kernels, body(): pl.pallas_call(main_kernel, out_shape=(shape(*planes), shape(4, 256), sha...  4.19 us
    ppermute x1, starting transfers between devices, body(): below = lax.ppermute(up, 'gz', ahead)  1.92 us
    pallas_call x1, Pallas kernels, body(): pl.pallas_call(prepare_kernel, in_specs=[pl.BlockSpec(memory_space=pltpu....  1.88 us
  transfers between devices with their start and end apart: 2, of which 1 were waited for; matrix products, arithmetic and copies ran while one was open for 0% of the time, Pallas kernels for 3%

profile of v2, /device:TPU:1, one launch (start us, length us, event | category | flops | bytes accessed | tf_op | source)
XLA Modules:
  0.0 67.4 jit_solution(16818222736695410190)
XLA Ops:
  0.6 1.0 %sites.1 = (f32[4,128]{1,0:T(4,128)S(1)}, f32[4,128]{1,0:T(4,128)S(1)}, f32[4,128]{1,0:T(4,128)S(1)}, bf16[72,128]{1,0:T(8,128)(2,1)S(1)}) custom-call(f32[3,1,72]{2,1,0:T(1,128)} %bitcast.17, s32[1,72]{1,0:T(1,128)} %refs_3_.1, s32[1,72]{1,0:T(1,128)} %site_hbm.1), custom_call_target="tpu_custom_call" | custom-call | tf_op jit(solution)/shard_map/sites/pallas_call | solution.py:680
  1.6 11.5 %collective-permute-start.1 = (f32[4,128]{1,0:T(4,128)S(1)}, f32[4,128]{1,0:T(4,128)S(1)}, u32[]{:S(2)}, u32[]{:S(2)}) collective-permute-start(f32[4,128]{1,0:T(4,128)S(1)} %get-tuple-element.32.down_ref), channel_id=1, source_target_pairs={{1,0},{2,1},{3,2},{4,3},{5,4},{6,5},{7,6},{0,7},{9,8},{10,9},{11,1... | collective-permute-start | bytes 6152 | tf_op jit(solution)/shard_map/ppermute | solution.py:696
  13.2 1.9 %collective-permute-start = (f32[4,128]{1,0:T(4,128)S(1)}, f32[4,128]{1,0:T(4,128)S(1)}, u32[]{:S(2)}, u32[]{:S(2)}) collective-permute-start(f32[4,128]{1,0:T(4,128)S(1)} %get-tuple-element.33.up_ref), channel_id=1, source_target_pairs={{0,1},{1,2},{2,3},{3,4},{4,5},{5,6},{6,7},{7,0},{8,9},{9,10},{10,1... | collective-permute-start | bytes 6152 | tf_op jit(solution)/shard_map/ppermute | solution.py:695
  15.7 1.9 %slots_and_weights.1 = (s32[1,1152]{1,0:T(1,128)S(1)}, f32[1,1152]{1,0:T(1,128)S(1)}, f32[8,256]{1,0:T(8,128)S(1)}, f32[8,256]{1,0:T(8,128)S(1)}, bf16[128,48]{1...) custom-call(s32[1]{0:T(128)S(6)} %copy.22.count_ref, ...), custom_call_target="tpu_custom_call" | custom-call | flops 10000000 | bytes 2000000 | tf_op jit(solution)/shard_map/slots_and_weights/pallas_call | solution.py:712
  17.6 0.0 collective-permute-done.1.above_ref
  17.6 1.1 %collective-permute-done.below_ref = f32[4,128]{1,0:T(4,128)S(1)} collective-permute-done((f32[4,128]{1,0:T(4,128)S(1)}, f32[4,128]{1,0:T(4,128)S(1)}, u32[]{:S(2)}, u32[]{:S(2)}) %collective-permute-start) | collective-permute-done | bytes 2080 | tf_op jit(solution)/shard_map/ppermute | solution.py:695
  18.7 0.2 column.1
  18.9 21.2 %all_to_all.27 = f32[64,1,128]{2,1,0:T(1,128)S(1)} all-to-all(f32[64,1,128]{2,1,0:T(1,128)S(1)} %bitcast.15), channel_id=1, replica_groups=mesh['gx'=8,'gy'=8,'gz'=8] {'gx','gy'}, dimensions={0} | all-to-all | bytes 65536 | tf_op jit(solution)/shard_map/all_to_all | solution.py:745
  40.1 4.2 %edges.1 = (f32[64,128]{1,0:T(8,128)S(1)}, f32[4,256]{1,0:T(4,128)S(1)}, f32[8,72]{1,0:T(8,128)S(1)}) custom-call(f32[64,128]{1,0:T(8,128)S(1)} %bitcast.12, f32[4,128]{1,0:T(4,128)S(1)} %get-tuple-element.36.outer_ref, f32[4,128]{1,0:T(4,128)S(1)} %get-tuple-element.37.inner_ref, s32[1,1152]{1,0:T(1,128)S(1)} %get-tuple-element.38.cell_ref, ...), custom_call_target="tpu_custom_call" | custom-call | tf_op jit(solution)/shard_map/edges/pallas_call | solution.py:747
  44.3 13.1 %all_to_all.28 = f32[64,1,128]{2,1,0:T(1,128)S(1)} all-to-all(f32[64,1,128]{2,1,0:T(1,128)S(1)} %bitcast.14), channel_id=1, replica_groups=mesh['gx'=8,'gy'=8,'gz'=8] {'gx','gy'}, dimensions={0} | all-to-all | bytes 65536 | tf_op jit(solution)/shard_map/all_to_all | solution.py:769
  57.4 0.2 columns_back.1
  57.6 9.0 %all_to_all.29.recv_ref = f32[8,4,128]{2,1,0:T(4,128)S(1)} all-to-all(f32[8,4,128]{2,1,0:T(4,128)S(1)} %get-tuple-element.54), channel_id=1, replica_groups=mesh['gx'=8,'gy'=8,'gz'=8] {'gz'}, dimensions={0} | all-to-all | bytes 32768 | tf_op jit(solution)/shard_map/all_to_all | solution.py:776
  66.6 0.8 %forces.1 = (f32[3,1,72]{2,1,0:T(1,128)}, f32[1,72]{1,0:T(1,128)}, f32[3,3]{1,0:T(4,128)}) custom-call(f32[8,4,128]{2,1,0:T(4,128)S(1)} %all_to_all.29.recv_ref, f32[8,128]{1,0:T(8,128)S(1)} %get-tuple-element.55.keep_ref, f32[8,72]{1,0:T(8,128)S(1)} %get-tuple-element.56.local_ref, bf16[72,128]{1,0:T(8,128)(2,1)S(1)} %get-tuple-element.57.hot_ref), custom_call_target="tpu_custom_call" | custom-call | tf_op jit(solution)/shard_map/forces/pallas_call | solution.py:777
Async XLA Ops:
  1.6 16.0 %collective-permute-start.1 = (f32[4,128]{1,0:T(4,128)S(1)}, f32[4,128]{1,0:T(4,128)S(1)}, u32[]{:S(2)}, u32[]{:S(2)}) collective-permute-start(f32[4,128]{1,0:T(4,128)S(1)} %get-tuple-element.32.down_ref), channel_id=1, source_target_pairs={{1,0},{2,1},{3,2},{4,3},{5,4},{6,5},{7,6},{0,7},{9,8},{10,9},{11,1... | collective-permute-start | bytes 6152 | tf_op jit(solution)/shard_map/ppermute | solution.py:696
  13.2 5.5 %collective-permute-start = (f32[4,128]{1,0:T(4,128)S(1)}, f32[4,128]{1,0:T(4,128)S(1)}, u32[]{:S(2)}, u32[]{:S(2)}) collective-permute-start(f32[4,128]{1,0:T(4,128)S(1)} %get-tuple-element.33.up_ref), channel_id=1, source_target_pairs={{0,1},{1,2},{2,3},{3,4},{4,5},{5,6},{6,7},{7,0},{8,9},{9,10},{10,1... | collective-permute-start | bytes 6152 | tf_op jit(solution)/shard_map/ppermute | solution.py:695

commit v3 on v2

--- a/solution.py
+++ b/solution.py
@@ -24,76 +24,24 @@
 STEPS = [(dx, dy) for dx in (-1, 0, 1) for dy in (-1, 0, 1) if (dx, dy) != (0, 0)]
 
 
-RIM_SITES = (
-    [(0, y) for y in range(6)]
-    + [(5, y) for y in range(6)]
-    + [(x, 0) for x in range(1, 5)]
-    + [(x, 5) for x in range(1, 5)]
-)
-
-
-def ring_index(i, j):
-    if i == 0:
-        return j
-    if i == 7:
-        return 8 + j
-    if j == 0:
-        return 16 + i - 1
-    return 22 + i - 1
-
-
-def cell_number(i, j, k):
-    if i in (0, 7) or j in (0, 7):
-        return k * RING + ring_index(i, j)
-    return 112 + k * 36 + (i - 1) * 6 + (j - 1)
-
-
 SITE_RANGE = {1: [5], -1: [0], 0: list(range(6))}
-CELL_RANGE = {1: [7], -1: [0], 0: list(range(1, 7))}
-
-
-def face(ranges, dx, dy):
-    return list(enumerate((a, b) for a in ranges[dx] for b in ranges[dy]))
+def face(dx, dy):
+    return list(enumerate((x, y) for x in SITE_RANGE[dx] for y in SITE_RANGE[dy]))
 
 
 def tables():
-    send_sites = np.full((8, 4, 4, 8), -1, np.int32)
-    send_cells = np.full((8, 4, 4, 8), -1, np.int32)
-    source = np.full((256,), -1, np.int32)
-    target = np.full((10 * LANES,), -1, np.int32)
-    places = {0: 0, 3: 64, 1: LANES, 2: LANES + 64}
-    landing = target[: 8 * LANES].reshape(8, 4, 4, 8)
-    for n, (dx, dy) in enumerate(STEPS):
-        for at, site in face(SITE_RANGE, dx, dy):
-            for k in range(4):
-                send_sites[n, :, k, at] = k * 32 + RIM_SITES.index(site)
-        for at, (i, j) in face(CELL_RANGE, dx, dy):
-            for k in range(4):
-                send_cells[n, :3, k, at] = cell_number(i, j, k)
-        for at, (x, y) in face(SITE_RANGE, -dx, -dy):
-            i = {1: 7, -1: 0, 0: x + 1}[dx]
-            j = {1: 7, -1: 0, 0: y + 1}[dy]
-            for k in range(4):
-                source[cell_number(i, j, k)] = n * LANES + k * 8 + at
-        for at, (i, j) in face(CELL_RANGE, -dx, -dy):
-            x = {1: 5, -1: 0, 0: i - 1}[dx]
-            y = {1: 5, -1: 0, 0: j - 1}[dy]
-            for k in range(4):
-                landing[n, :3, k, at] = places[k] + x * 6 + y
-    for x in range(CELLS):
-        for y in range(CELLS):
-            for k in range(4):
-                own = cell_number(x + 1, y + 1, k)
-                source[own] = 8 * LANES + places[k] + x * 6 + y
-                target[8 * LANES + own] = places[k] + x * 6 + y
-    row = np.arange(10 * LANES)[:, None]
-    forward = np.where(row < 8 * LANES, row & ~96, row) == source
-    back = target[:, None] == np.arange(256)
-    lane = np.arange(LANES)[:, None]
-    return forward, back, lane == send_sites.reshape(-1), lane == send_cells.reshape(-1)
-
-
-TABLES = tables()
+    routes = np.zeros((512, 256), np.float32)
+    layers = {0: 0, 3: 64, 1: LANES, 2: LANES + 64}
+    for k in range(4):
+        for n, (dx, dy) in enumerate(STEPS):
+            for m, (x, y) in face(dx, dy):
+                place, column = n * 32 + k * 8 + m, layers[k] + x * 6 + y
+                routes[column, place] = 1.0
+                routes[256 + place, column] = 1.0
+    return routes
+
+
+ROUTES = tables()
 
 
 def parts_of(x, count):
@@ -141,53 +89,79 @@
     return copies
 
 
-def fetch(sources, buffers, sems):
-    for copy in start_fetch(sources, buffers, sems):
-        copy.wait()
-
-
 def atom_rows(pos_ref, kind_ref):
     kind = kind_ref[...].astype(F32)
     return jnp.concatenate([pos_ref[0], pos_ref[1], pos_ref[2], kind, jnp.zeros((4, ATOMS), F32)], axis=0)
 
 
 def lane_sites():
-    lane = iota((8, 3 * LANES), 1)
-    part, at = lane >> 7, lane & 63
-    second = (lane & 64) > 0
-    rim = jnp.where(
-        at < 12,
-        jnp.where(at < 6, at, 24 + at),
-        jnp.where(at < 16, 6 * (at - 11), 6 * (at - 15) + 5),
-    )
-    whole = jnp.where(at < 36, at, 1000)
-    rim = jnp.where(at < 20, rim, 1000)
-    layer = jnp.where(part == 0, jnp.where(second, 1, 0), part - 1)
-    return 2 * jnp.where((part > 0) & second, rim, whole) + layer
-
-
-def send_kernel(pos_hbm, kind_hbm, site_hbm, both_ref, down_ref, up_ref, hot_ref, pos_ref, kind_ref, site_ref, sems):
-    fetch((pos_hbm, kind_hbm, site_hbm), (pos_ref, kind_ref, site_ref), sems)
+    lane = iota((8, LANES), 1)
+    at = lane & 63
+    return jnp.where(at < 36, 2 * at + (lane >> 6), -1)
+
+
+def low_half(x, y):
+    return jnp.where(iota(x.shape, 1) < 64, x, y)
+
+
+def even_layer():
+    return (lax.axis_index("gz") & 1) == 0
+
+
+def send_kernel(*refs):
+    sources, (both_ref, first_ref, second_ref, hot_ref), copied = refs[:13], refs[13:17], refs[17:29]
+    pos_ref, kind_ref, site_ref = copied[0], copied[1], refs[29]
+    copies = start_fetch(sources, (site_ref,) + copied, refs[30])
+    for copy in copies[:3]:
+        copy.wait()
     rows = atom_rows(pos_ref, kind_ref)
     hot = as_hot(iota((ATOMS, ATOMS), 0) == site_ref[...])
-    pick = as_hot(iota((ATOMS, 3 * LANES), 0) == lane_sites()[0:1])
+    pick = as_hot(iota((ATOMS, LANES), 0) == lane_sites()[0:1])
     placed = jnp.dot(hot, pick, preferred_element_type=F32).astype(BF16)
-    out = exact_dot(rows, placed)
-    both_ref[...] = out[:4, 0:LANES]
-    down_ref[...] = out[:4, LANES : 2 * LANES]
-    up_ref[...] = out[:4, 2 * LANES : 3 * LANES]
-    hot_ref[...] = placed[:, 0:LANES]
-
-
-def by_component(row):
-    lane, comp = iota((8, LANES), 1), iota((8, LANES), 0)
-    return jnp.where((lane >> 5) == comp, jnp.broadcast_to(row, (8, LANES)), 0.0)
-
-
-def to_rows(x, table):
-    out = exact_dot(x, table)
-    keep = ((iota(out.shape, 1) >> 5) & 3) == iota(out.shape, 0)
-    return jnp.sum(jnp.where(keep, out, 0.0), axis=0, keepdims=True)
+    both = exact_dot(rows, placed)
+    turned = pltpu.roll(both, 64, 1)
+    down = [low_half(both[c : c + 1], turned[c + 1 : c + 2]) for c in (0, 2)]
+    up = [low_half(turned[c : c + 1], both[c + 1 : c + 2]) for c in (0, 2)]
+    for c in range(2):
+        first_ref[c : c + 1] = jnp.where(even_layer(), down[c], up[c])
+        second_ref[c : c + 1] = jnp.where(even_layer(), up[c], down[c])
+    both_ref[...] = both[:4]
+    hot_ref[...] = placed
+    for copy in copies[3:]:
+        copy.wait()
+
+
+def on_component():
+    return (iota((8, LANES), 1) >> 5) == iota((8, LANES), 0)
+
+
+def turn(x, step):
+    comp = iota((8, LANES), 0)
+    out = x
+    for c in range(1, 4):
+        out = jnp.where(comp == c, pltpu.roll(x, c * step % LANES, 1), out)
+    return out
+
+
+def from_rows(rows):
+    halves = []
+    for h in range(2):
+        total = jnp.zeros((8, LANES), F32)
+        for m in range(4):
+            part = jnp.where(on_component(), jnp.broadcast_to(rows[4 * h + m], (8, LANES)), 0.0)
+            total = total + (pltpu.roll(part, 32 * m, 1) if m else part)
+        halves.append(turn(total, -32))
+    return halves
+
+
+def to_rows(x):
+    rows = []
+    for h in range(2):
+        turned = turn(x[:, h * LANES : (h + 1) * LANES], 32)
+        for m in range(4):
+            part = pltpu.roll(turned, LANES - 32 * m, 1) if m else turned
+            rows.append(jnp.sum(jnp.where(on_component(), part, 0.0), axis=0, keepdims=True))
+    return rows
 
 
 def neighbour(n):
@@ -197,80 +171,68 @@
     return lax.rem(gx + (dx + COUNT), COUNT) * COUNT + lax.rem(gy + (dy + COUNT), COUNT)
 
 
-def column_kernel(down_ref, up_ref, below_ref, above_ref, table_ref, msg_ref, outer_ref):
-    lane = iota((8, LANES), 1)
-
-    def rim(x, at):
-        return pltpu.roll(x, (at - 64) % LANES, 1)
-
-    below, above, low, high = (pad_rows(ref[...]) for ref in (below_ref, above_ref, down_ref, up_ref))
-    column = jnp.where(
-        lane < 32,
-        rim(below, 0),
-        jnp.where(lane < 64, rim(low, 32), jnp.where(lane < 96, rim(high, 64), rim(above, 96))),
-    )
-    outer_ref[...] = jnp.where(lane < 64, below, pltpu.roll(above, 64, 1))[:4]
-    rows = to_rows(column, table_ref[...])
+def column_kernel(inner_ref, first_ref, second_ref, routes_ref, tie_ref, msg_ref, outer_ref):
+    first, second = first_ref[...], second_ref[...]
+    below = jnp.where(even_layer(), first, second)
+    above = jnp.where(even_layer(), second, first)
+    below_turned, above_turned = pltpu.roll(below, 64, 1), pltpu.roll(above, 64, 1)
+    rows = []
+    for c in range(2):
+        at = slice(c, c + 1)
+        rows += [low_half(below[at], above_turned[at]), low_half(below_turned[at], above[at])]
+    outer = pad_rows(jnp.concatenate(rows, axis=0))
+    outer_ref[...] = outer[:4]
+    column = jnp.concatenate([outer, pad_rows(inner_ref[...])], axis=1)
+    rows = to_rows(exact_dot(column, routes_ref[:256]))
     msg_ref[...] = jnp.zeros_like(msg_ref)
     for n in range(8):
-        msg_ref[pl.ds(neighbour(n), 1), :] = rows[:, n * LANES : (n + 1) * LANES]
+        msg_ref[pl.ds(neighbour(n), 1), :] = rows[n]
 
 
 def cat_of(w):
     high = w.astype(BF16).astype(F32)
     low = w - high
-    return jnp.concatenate([high, high, low], axis=1).astype(BF16)
+    both = jnp.concatenate([high, low], axis=0)
+    return jnp.concatenate([both, both], axis=1).astype(BF16)
+
+
+def dot_cat(w, x):
+    out = jnp.dot(w, x, preferred_element_type=F32)
+    rows = out.shape[0] // 2
+    return out[:rows] + out[rows:]
 
 
 def cell_shifts():
-    lane = iota((8, 256), 1)
-    row = iota((8, 256), 0)
-    inside = lane - 112
-    ring_layer = jnp.where(lane >= 28, 1, 0) + jnp.where(lane >= 56, 1, 0) + jnp.where(lane >= 84, 1, 0)
-    ring = lane - 28 * ring_layer
-    outer = lane < 112
-    layer = jnp.where(
-        outer,
-        ring_layer,
-        jnp.where(inside >= 36, 1, 0) + jnp.where(inside >= 72, 1, 0) + jnp.where(inside >= 108, 1, 0),
-    )
-    low_z = layer == 0
-    high_z = layer == 3
-    corner_low = (ring == 0) | (ring == 8)
-    corner_high = (ring == 7) | (ring == 15)
-    low_y = outer & (corner_low | ((ring >= 16) & (ring < 22)))
-    high_y = outer & (corner_high | (ring >= 22))
-    low_x = outer & (ring < 8)
-    high_x = outer & (ring >= 8) & (ring < 16)
-
-    def sides(low, high, edge):
-        return jnp.where(high, edge, 0.0) - jnp.where(low, edge, 0.0)
-
-    return jnp.where(
-        row == 0,
-        sides(low_x, high_x, 12.0),
-        jnp.where(row == 1, sides(low_y, high_y, 12.0), jnp.where(row == 2, sides(low_z, high_z, 4.0), 0.0)),
-    )
+    lane = iota((8, 512), 1)
+    row = iota((8, 512), 0)
+    outer = lane < 256
+    code = lane >> 5
+    code = code + jnp.where(code >= 4, 1, 0)
+    third = jnp.where(code >= 3, 1, 0) + jnp.where(code >= 6, 1, 0)
+    along_x = jnp.where(outer, third - 1, 0)
+    along_y = jnp.where(outer, code - 3 * third - 1, 0)
+    layer = (lane >> 3) & 3
+    part = lane >> 6
+    low_z = jnp.where(outer, layer, part - 4) == 0
+    high_z = jnp.where(outer, layer, part - 2) == 3
+    along_z = jnp.where(high_z, 1, 0) - jnp.where(low_z, 1, 0)
+    shift = jnp.where(row == 0, 12 * along_x, jnp.where(row == 1, 12 * along_y, 4 * along_z))
+    return jnp.where(row < 3, shift, 0).astype(F32)
 
 
 def prepare_kernel(count_ref, *refs):
-    sources, outputs, buffers, sems = refs[:15], refs[15:30], refs[30:41], refs[41]
-    copies = start_fetch(sources, buffers + outputs[11:], sems)
-    make_slots(count_ref, copies[:4], buffers[:4], outputs[:4])
-    make_weights(copies[4:11], buffers[4:], outputs[4:11])
-    for copy in copies[11:]:
-        copy.wait()
-
-
-def make_slots(count_ref, copies, buffers, outputs):
-    center_ref, other_ref, pos_ref, kind_ref = buffers
+    inputs, outputs = refs[:11], refs[11:]
+    make_slots(count_ref, inputs[:4], outputs[:4])
+    make_weights(inputs[4:], outputs[4:])
+
+
+def make_slots(count_ref, buffers, outputs):
+    pos_ref, kind_ref, center_ref, other_ref = buffers
     cell_ref, live_ref, own_ref, shift_ref = outputs
     shift_ref[...] = cell_shifts()
     before = as_hot((iota((LANES, 256), 0) < iota((LANES, 256), 1)) | (iota((LANES, 256), 1) >= LANES))
     lane = iota((ATOMS, 256), 1)
     spread = as_hot(iota((ATOMS, 256), 0) == jnp.where(lane < LANES, lane & 63, MAIN + (lane & 7)))
-    for copy in copies:
-        copy.wait()
     center = center_ref[...]
     other = other_ref[...]
     atom = lax.broadcasted_iota(jnp.int32, (ATOMS, EDGES), 0)
@@ -288,29 +250,34 @@
     block = jnp.where(is_main, rank >> 1, BLOCKS - 1)
     lane = jnp.where(is_main, (rank & 1) * MAIN + center, rank * 8 + (center - MAIN))
     i, j, k = other >> 5, (other >> 2) & 7, other & 3
-    ring = jnp.where(
-        i == 0, j, jnp.where(i == 7, 8 + j, jnp.where(j == 0, 15 + i, jnp.where(j == 7, 21 + i, -1)))
-    )
-    cell = jnp.where(ring >= 0, k * RING + ring, 112 + k * 36 + (i - 1) * 6 + (j - 1)).astype(F32)
+    dx = jnp.where(i == 7, 1, 0) - jnp.where(i == 0, 1, 0)
+    dy = jnp.where(j == 7, 1, 0) - jnp.where(j == 0, 1, 0)
+    code = 3 * dx + dy + 4
+    place = jnp.where(dx == 0, i - 1, 0) + jnp.where(dy == 0, j - 1, 0)
+    layer = jnp.where(k == 3, 64, jnp.where(k > 0, 64 * k + 64, 0))
+    cell = jnp.where(
+        code == 4,
+        256 + layer + (i - 1) * 6 + (j - 1),
+        (code - jnp.where(code > 4, 1, 0)) * 32 + k * 8 + place,
+    )
     slot = lax.broadcasted_iota(jnp.int32, (1, EDGES), 1)
     live = jnp.where(slot < count_ref[0], 1.0, 0.0)
     row = lax.broadcasted_iota(jnp.int32, (16, EDGES), 0)
-    left = jnp.concatenate([jnp.where(row == block, cell, 0.0), jnp.where(row == block, live, 0.0)], axis=0)
+    values = ((cell & 255).astype(F32), (cell >> 8).astype(F32), live)
+    left = jnp.concatenate([jnp.where(row == block, v, 0.0) for v in values], axis=0)
     lane_hot = jnp.where(lax.broadcasted_iota(jnp.int32, (LANES, EDGES), 0) == lane, 1.0, 0.0).astype(BF16)
     placed = lax.dot_general(
         left.astype(BF16), lane_hot, (((1,), (1,)), ((), ())), preferred_element_type=F32
     )
     for b in range(BLOCKS):
         at = slice(b * LANES, (b + 1) * LANES)
-        cell_ref[:, at] = placed[b : b + 1].astype(jnp.int32)
-        live_ref[:, at] = placed[16 + b : 17 + b]
+        cell_ref[:, at] = (placed[b : b + 1] + 256.0 * placed[16 + b : 17 + b]).astype(jnp.int32)
+        live_ref[:, at] = placed[32 + b : 33 + b]
     own_ref[...] = exact_dot(atom_rows(pos_ref, kind_ref), spread)
 
 
-def make_weights(copies, buffers, outputs):
+def make_weights(buffers, outputs):
     win_ref, w3_ref, wlat_ref, wlat_t_ref, w3_t_ref, win_t_ref, read_ref = outputs
-    for copy in copies:
-        copy.wait()
     w_in_ref, w_two_ref, w_env_ref, w_value_ref, w_latent_ref, w_out_ref, readout_ref = buffers
     w_in_t = w_in_ref[...]
     win_ref[...] = cat_of(w_in_t.T)
@@ -366,7 +333,6 @@
     low = (x - high.astype(F32)).astype(BF16)
     ref[pl.ds(row, 16), at] = high
     ref[pl.ds(depth + row, 16), at] = low
-    ref[pl.ds(2 * depth + row, 16), at] = high
 
 
 def repeat(count, step):
@@ -389,8 +355,6 @@
     w3_t_ref,
     win_t_ref,
     read_ref,
-    forward_ref,
-    cells_ref,
     msg_ref,
     ext_ref,
     local_ref,
@@ -411,11 +375,10 @@
 ):
     blocks = [slice(b * LANES, (b + 1) * LANES) for b in range(BLOCKS)]
 
-    columns = [by_component(recv_ref[pl.ds(neighbour(n), 1), :]) for n in range(8)]
+    columns = from_rows([recv_ref[pl.ds(neighbour(n), 1), :] for n in range(8)])
     columns += [pad_rows(outer_ref[...]), pad_rows(inner_ref[...])]
-    arrived = jnp.concatenate(columns, axis=1)
-    extended = exact_dot(arrived, forward_ref[...]) + shift_ref[...]
-    cells = lax.broadcasted_iota(jnp.int32, (256, EDGES), 0)
+    extended = jnp.concatenate(columns, axis=1) + shift_ref[...]
+    cells = lax.broadcasted_iota(jnp.int32, (512, EDGES), 0)
     hot[...] = jnp.where(cells == cell_ref[...], 1.0, 0.0).astype(BF16)
     partner = exact_dot(extended, hot[...])
     own = own_ref[...]
@@ -448,11 +411,7 @@
     inputs = jnp.concatenate([radial, one_hot], axis=0)
     inputs_high = inputs.astype(BF16)
     inputs_low = (inputs - inputs_high.astype(F32)).astype(BF16)
-    pre[0:16] = jnp.dot(
-        win_ref[...],
-        jnp.concatenate([inputs_high, inputs_low, inputs_high], axis=0),
-        preferred_element_type=F32,
-    ).reshape(16, 8, EDGES)
+    pre[...] = dot_cat(win_ref[...], jnp.concatenate([inputs_high, inputs_low], axis=0)).reshape(16, 8, EDGES)
 
     def first_layer(c, carry):
         v = pre[pl.ds(2 * c, 2)]
@@ -463,7 +422,7 @@
         return carry
 
     repeat(8, first_layer)
-    mixed[...] = jnp.dot(w3_ref[...], cat_a[0:384], preferred_element_type=F32).reshape(24, 8, EDGES)
+    mixed[...] = dot_cat(w3_ref[...], cat_a[...]).reshape(24, 8, EDGES)
 
     def forward_tile(t, carry):
         sums = [[None, None] for _ in range(9)]
@@ -497,7 +456,7 @@
         return carry
 
     repeat(4, forward_tile)
-    pre[...] = jnp.dot(wlat_ref[...], cat_b[...], preferred_element_type=F32).reshape(16, 8, EDGES)
+    pre[...] = dot_cat(wlat_ref[...], cat_b[...]).reshape(16, 8, EDGES)
     energy[...] = jnp.zeros((8, EDGES), F32)
 
     def second_layer(c, carry):
@@ -513,7 +472,7 @@
         return carry
 
     repeat(8, second_layer)
-    grad_lat[...] = jnp.dot(wlat_t_ref[...], cat_a[...], preferred_element_type=F32).reshape(32, 8, EDGES)
+    grad_lat[...] = dot_cat(wlat_t_ref[...], cat_a[...]).reshape(32, 8, EDGES)
     grad_harm[...] = jnp.zeros((8, 8, EDGES), F32)
     grad_env[...] = jnp.zeros((8, EDGES), F32)
 
@@ -561,7 +520,7 @@
         return carry
 
     repeat(4, backward_tile)
-    pre[...] = jnp.dot(w3_t_ref[...], cat_b[0:576], preferred_element_type=F32).reshape(16, 8, EDGES)
+    pre[...] = dot_cat(w3_t_ref[...], cat_b[0:384]).reshape(16, 8, EDGES)
 
     def first_back(c, carry):
         back = pre[pl.ds(2 * c, 2)] * slope[pl.ds(2 * c, 2)]
@@ -569,7 +528,7 @@
         return carry
 
     repeat(8, first_back)
-    d_radial = jnp.dot(win_t_ref[...], cat_a[...], preferred_element_type=F32)[:8]
+    d_radial = dot_cat(win_t_ref[...], cat_a[...])[:8]
 
     x, y, z = harm[0], harm[1], harm[2]
     scaled = x * x + y * y + z * z
@@ -583,8 +542,8 @@
     d_y = g[1] + ROOT3 * (x * g[3] + z * g[4] - y * g[6]) - y * g[7] + twice * y
     d_z = g[2] + ROOT3 * (y * g[4] + x * g[5]) + 2.0 * z * g[7] + twice * z
     e = energy[...] * env_live[...]
-    rows = [jnp.sum(v, axis=0, keepdims=True) for v in (d_x * 0.2, d_y * 0.2, d_z * 0.2, e)]
-    grads = jnp.concatenate(rows + [jnp.zeros((4, EDGES), F32)], axis=0)
+    partial = [d_x * 0.2, d_y * 0.2, d_z * 0.2]
+    extended_grad = exact_dot_nt(jnp.concatenate(partial, axis=0), hot[...], 2)
 
     def over_blocks(v):
         total = v[:, blocks[0]]
@@ -592,30 +551,37 @@
             total = total + v[:, blocks[b]]
         return total
 
-    main, last = sum_slots(over_blocks(grads), grads[:, blocks[8]])
-    atoms = jnp.concatenate([main[:, :MAIN], last[:, : ATOMS - MAIN]], axis=1)
-    local_ref[...] = atoms
-
-    extended_grad = exact_dot_nt(grads, hot[...])
-    ext_ref[...] = extended_grad[:4]
+    def summed(arrays):
+        rows = [jnp.sum(v, axis=0, keepdims=True) for v in arrays]
+        return jnp.concatenate(rows + [jnp.zeros((8 - len(rows), rows[0].shape[1]), F32)], axis=0)
+
+    virial = []
+    for a, comp in enumerate((x, y, z)):
+        for b in range(3):
+            product = comp * partial[b]
+            virial.append(over_blocks(product) + product[:, blocks[8]])
+    totals = jnp.sum(jnp.concatenate(virial, axis=0), axis=1, keepdims=True)
     lane = lax.broadcasted_iota(jnp.int32, (8, LANES), 1)
-    row = lax.broadcasted_iota(jnp.int32, (8, LANES), 0)
     virial = jnp.zeros((8, LANES), F32)
-    for a, comp in enumerate((x, y, z)):
-        product = comp * grads
-        total = jnp.sum(over_blocks(product) + product[:, blocks[8]], axis=1, keepdims=True)
-        virial = jnp.where((lane == 96 + row + 3 * a) & (row < 3), total * 5.0, virial)
+    for n in range(9):
+        virial = jnp.where(lane == 96 + n, totals[8 * n : 8 * n + 8] * 5.0, virial)
     virial = jnp.sum(virial, axis=0, keepdims=True)
-    rows = to_rows(extended_grad[:, :LANES], cells_ref[...])
+
+    extended_grad = summed([extended_grad[8 * c : 8 * c + 8] for c in range(3)])
+    rows = to_rows(extended_grad[:, :256])
     msg_ref[...] = jnp.broadcast_to(virial, (COUNT * COUNT, LANES))
     for n in range(8):
-        msg_ref[pl.ds(neighbour(n), 1), :] = rows[:, n * LANES : (n + 1) * LANES] + virial
-
-
-def middle_kernel(recv_ref, ext_ref, back_ref, msg_ref, keep_ref):
-    columns = [by_component(recv_ref[pl.ds(neighbour(n), 1), :]) for n in range(8)]
-    arrived = jnp.concatenate(columns + [pad_rows(ext_ref[...])], axis=1)
-    sums = exact_dot(arrived, back_ref[...])
+        msg_ref[pl.ds(neighbour(n), 1), :] = rows[n] + virial
+    ext_ref[...] = extended_grad[:4, 256:]
+
+    arrays = partial + [e]
+    main, last = sum_slots(summed([over_blocks(v) for v in arrays]), summed([v[:, blocks[8]] for v in arrays]))
+    local_ref[...] = jnp.concatenate([main[:, :MAIN], last[:, : ATOMS - MAIN]], axis=1)
+
+
+def middle_kernel(recv_ref, ext_ref, routes_ref, msg_ref, keep_ref):
+    columns = from_rows([recv_ref[pl.ds(neighbour(n), 1), :] for n in range(8)])
+    sums = exact_dot(jnp.concatenate(columns, axis=1), routes_ref[256:], 2) + pad_rows(ext_ref[...])
     total = jnp.sum(recv_ref[...], axis=0, keepdims=True)
     message = jnp.concatenate([sums[:3, :LANES], total], axis=0)
     msg_ref[...] = jnp.broadcast_to(message[None], (COUNT, 4, LANES))
@@ -629,7 +595,7 @@
     lane = lax.broadcasted_iota(jnp.int32, (8, LANES), 1)
     row = lax.broadcasted_iota(jnp.int32, (8, LANES), 0)
     sites = keep_ref[...] + jnp.where(lane < 64, pltpu.roll(below, 64, 1), pltpu.roll(above, 64, 1))
-    atoms = exact_dot_nt(sites, hot_ref[...])
+    atoms = exact_dot_nt(sites, hot_ref[...], 2)
     energy_ref[...] = local_ref[3:4]
     force = local_ref[...] - atoms
     for comp in range(3):
@@ -649,10 +615,6 @@
 
 def in_hbm(*arrays):
     return [pltpu.with_memory_space_constraint(x, pltpu.HBM) for x in arrays]
-
-
-def fetched(arrays, more=0):
-    return [pltpu.VMEM(x.shape, x.dtype) for x in arrays] + [pltpu.SemaphoreType.DMA((len(arrays) + more,))]
 
 
 def params():
@@ -676,30 +638,12 @@
 ):
     half = (4, LANES)
     hbm = pl.BlockSpec(memory_space=pltpu.HBM)
-    columns_first = jnp.transpose(positions, (1, 0, 2))
-    own, down, up, hot = pl.pallas_call(
-        send_kernel,
-        in_specs=[hbm] * 3,
-        out_shape=(shape(*half), shape(*half), shape(*half), shape(ATOMS, LANES, dtype=BF16)),
-        scratch_shapes=[
-            pltpu.VMEM((3, 1, ATOMS), F32),
-            pltpu.VMEM((1, ATOMS), jnp.int32),
-            pltpu.VMEM((1, ATOMS), jnp.int32),
-            pltpu.SemaphoreType.DMA((3,)),
-        ],
-        compiler_params=params(),
-        name="sites",
-    )(*in_hbm(columns_first, species, site_atom))
-    ahead = [(i, (i + 1) % COUNT) for i in range(COUNT)]
-    behind = [(target, source) for source, target in ahead]
-    below = lax.ppermute(up, "gz", ahead)
-    above = lax.ppermute(down, "gz", behind)
-
     inputs = (
+        site_atom,
+        jnp.transpose(positions, (1, 0, 2)),
+        species,
         edge_center,
         edge_other,
-        columns_first,
-        species,
         w_in.T,
         w_two,
         w_env,
@@ -707,33 +651,41 @@
         w_latent,
         w_out,
         readout.reshape(1, 64),
-    )
-    routes = [jnp.asarray(table, BF16) for table in TABLES]
+        jnp.asarray(ROUTES, BF16),
+    )
+    own, first, second, hot, *copied, routes = pl.pallas_call(
+        send_kernel,
+        in_specs=[hbm] * len(inputs),
+        out_shape=(shape(*half), shape(2, LANES), shape(2, LANES), shape(ATOMS, LANES, dtype=BF16))
+        + tuple(shape(*x.shape, dtype=x.dtype) for x in inputs[1:]),
+        scratch_shapes=[pltpu.VMEM((1, ATOMS), jnp.int32), pltpu.SemaphoreType.DMA((len(inputs),))],
+        compiler_params=params(),
+        name="sites",
+    )(*in_hbm(*inputs))
+    first = lax.ppermute(first, "gz", [(i, ((i - 1) ^ 1) + 1 & 7) for i in range(COUNT)])
+    second = lax.ppermute(second, "gz", [(i, i ^ 1) for i in range(COUNT)])
+
+    vmem = pl.BlockSpec(memory_space=pltpu.VMEM)
     prepared = pl.pallas_call(
         prepare_kernel,
-        in_specs=[pl.BlockSpec(memory_space=pltpu.SMEM)] + [hbm] * (len(inputs) + 4),
+        in_specs=[pl.BlockSpec(memory_space=pltpu.SMEM)] + [vmem] * 11,
         out_shape=(
             shape(1, EDGES, dtype=jnp.int32),
             shape(1, EDGES),
             shape(8, 256),
-            shape(8, 256),
-            shape(128, 48, dtype=BF16),
-            shape(192, 384, dtype=BF16),
-            shape(128, 768, dtype=BF16),
+            shape(8, 512),
+            shape(256, 32, dtype=BF16),
+            shape(384, 256, dtype=BF16),
+            shape(256, 512, dtype=BF16),
+            shape(512, 256, dtype=BF16),
             shape(256, 384, dtype=BF16),
-            shape(128, 576, dtype=BF16),
-            shape(16, 384, dtype=BF16),
+            shape(32, 256, dtype=BF16),
             shape(128, LANES),
-            shape(10 * LANES, 256, dtype=BF16),
-            shape(10 * LANES, 256, dtype=BF16),
-            shape(LANES, 8 * LANES, dtype=BF16),
-            shape(LANES, 8 * LANES, dtype=BF16),
         ),
-        scratch_shapes=fetched(inputs, 4),
         compiler_params=params(),
         cost_estimate=pl.CostEstimate(flops=10_000_000, bytes_accessed=2_000_000, transcendentals=0),
         name="slots_and_weights",
-    )(edge_count, *in_hbm(*inputs, *routes))
+    )(edge_count, *copied)
 
     planes = (COUNT * COUNT, LANES)
     column, outer = pl.pallas_call(
@@ -741,20 +693,20 @@
         out_shape=(shape(*planes), shape(*half)),
         compiler_params=params(),
         name="column",
-    )(down, up, below, above, prepared[13])
+    )(own, first, second, routes, prepared[3])
     arrived = lax.all_to_all(column, ("gx", "gy"), 0, 0)
 
     message, extended_grad, local_grad = pl.pallas_call(
         main_kernel,
         out_shape=(shape(*planes), shape(4, 256), shape(8, ATOMS)),
         scratch_shapes=[
-            pltpu.VMEM((256, EDGES), BF16),
+            pltpu.VMEM((512, EDGES), BF16),
             pltpu.VMEM((8, 8, EDGES), F32),
             pltpu.VMEM((8, EDGES), F32),
             pltpu.VMEM((16, 8, EDGES), F32),
             pltpu.VMEM((16, 8, EDGES), F32),
-            pltpu.VMEM((384, EDGES), BF16),
-            pltpu.VMEM((768, EDGES), BF16),
+            pltpu.VMEM((256, EDGES), BF16),
+            pltpu.VMEM((512, EDGES), BF16),
             pltpu.VMEM((24, 8, EDGES), F32),
             pltpu.VMEM((2, 8, 8, EDGES), F32),
             pltpu.VMEM((9, 8, 8, 256), F32),
@@ -765,14 +717,14 @@
         ],
         compiler_params=params(),
         name="edges",
-    )(arrived, outer, own, *prepared[:12], prepared[14])
+    )(arrived, outer, own, *prepared)
     returned = lax.all_to_all(message, ("gx", "gy"), 0, 0)
     layers, keep = pl.pallas_call(
         middle_kernel,
         out_shape=(shape(COUNT, 4, LANES), shape(8, LANES)),
         compiler_params=params(),
         name="columns_back",
-    )(returned, extended_grad, prepared[12])
+    )(returned, extended_grad, routes)
     closing = lax.all_to_all(layers, "gz", 0, 0)
     forces, site_energy, virial = pl.pallas_call(
         last_kernel,

time: 67.7 us -> 67 us (0.990)
  Pallas kernels: 8.29 us -> 7.6 us
    pallas_call x1, Pallas kernels: 1.88 us -> 0.63 us  [body(): pl.pallas_call(prepare_kernel, in_specs=[pl.BlockSpec(memory_space=pltpu....]
  transfers between devices with their start and end apart: 2 -> 2, of which waited for: 1 -> 1; matrix products, arithmetic and copies ran while one was open for 0% -> 0% of each run, Pallas kernels for 3% -> 1%
where the time goes in v3:
time: 67 us; the launch traced here: 66.7 us
  blocking collectives  43.2 us (64%)
  starting transfers between devices  13.4 us (20%)
  Pallas kernels  7.6 us (11%)
  between operations  1.34 us (2%)
  waiting for transfers between devices  1.09 us (2%)
    all_to_all x1, blocking collectives, body(): arrived = lax.all_to_all(column, ('gx', 'gy'), 0, 0)  21.2 us
    all_to_all x1, blocking collectives, body(): returned = lax.all_to_all(message, ('gx', 'gy'), 0, 0)  13.1 us
    ppermute x1, starting transfers between devices, body(): lax.ppermute(first, 'gz', [(i, (i - 1 ^ 1) + 1 & 7) for i in range(COUNT)])  11.5 us
    all_to_all x1, blocking collectives, body(): closing = lax.all_to_all(layers, 'gz', 0, 0)  8.98 us
    pallas_call x1, Pallas kernels, body(): pl.pallas_call(main_kernel, out_shape=(shape(*planes), shape(4, 256), sha...  4.26 us
    ppermute x1, starting transfers between devices, body(): second = lax.ppermute(second, 'gz', [(i, i ^ 1) for i in range(COUNT)])  1.92 us
  transfers between devices with their start and end apart: 2, of which 1 were waited for; matrix products, arithmetic and copies ran while one was open for 0% of the time, Pallas kernels for 1%

profile of v3, /device:TPU:1, one launch (start us, length us, event | category | flops | bytes accessed | tf_op | source)
XLA Modules:
  0.0 66.7 jit_solution(17429647936395879395)
XLA Ops:
  0.6 1.3 %sites.1 = (f32[4,128]{1,0:T(4,128)S(1)}, f32[2,128]{1,0:T(2,128)S(1)}, f32[2,128]{1,0:T(2,128)S(1)}, bf16[72,128]{1,0:T(8,128)(2,1)S(1)}, f32[3,1,72]{2,1,0:T(1...) custom-call(s32[1,72]{1,0:T(1,128)} %refs_0_.1, ...), custom_call_target="tpu_custom_call" | custom-call | tf_op jit(solution)/shard_map/sites/pallas_call | solution.py:656
  2.0 11.5 %collective-permute-start = (f32[2,128]{1,0:T(2,128)S(1)}, f32[2,128]{1,0:T(2,128)S(1)}, u32[]{:S(2)}, u32[]{:S(2)}) collective-permute-start(f32[2,128]{1,0:T(2,128)S(1)} %get-tuple-element.41), channel_id=1, source_target_pairs={{0,7},{1,2},{2,1},{3,4},{4,3},{5,6},{6,5},{7,0},{8,15},{9,10},{10,... | collective-permute-start | bytes 3080 | tf_op jit(solution)/shard_map/ppermute | solution.py:665
  13.5 1.9 %collective-permute-start.1 = (f32[2,128]{1,0:T(2,128)S(1)}, f32[2,128]{1,0:T(2,128)S(1)}, u32[]{:S(2)}, u32[]{:S(2)}) collective-permute-start(f32[2,128]{1,0:T(2,128)S(1)} %get-tuple-element.42), channel_id=1, source_target_pairs={{0,1},{1,0},{2,3},{3,2},{4,5},{5,4},{6,7},{7,6},{8,9},{9,8},{10,11... | collective-permute-start | bytes 3080 | tf_op jit(solution)/shard_map/ppermute | solution.py:666
  16.0 0.6 slots_and_weights.1
  16.7 0.0 collective-permute-done.first_ref
  16.7 1.1 %collective-permute-done.1.second_ref = f32[2,128]{1,0:T(2,128)S(1)} collective-permute-done((f32[2,128]{1,0:T(2,128)S(1)}, f32[2,128]{1,0:T(2,128)S(1)}, u32[]{:S(2)}, u32[]{:S(2)}) %collective-permute-start.1) | collective-permute-done | bytes 1056 | tf_op jit(solution)/shard_map/ppermute | solution.py:666
  17.8 0.4 column.1
  18.1 21.2 %all_to_all.27 = f32[64,1,128]{2,1,0:T(1,128)S(1)} all-to-all(f32[64,1,128]{2,1,0:T(1,128)S(1)} %bitcast.15), channel_id=1, replica_groups=mesh['gx'=8,'gy'=8,'gz'=8] {'gx','gy'}, dimensions={0} | all-to-all | bytes 65536 | tf_op jit(solution)/shard_map/all_to_all | solution.py:697
  39.3 4.3 %edges.1 = (f32[64,128]{1,0:T(8,128)S(1)}, f32[4,256]{1,0:T(4,128)S(1)}, f32[8,72]{1,0:T(8,128)S(1)}) custom-call(f32[64,128]{1,0:T(8,128)S(1)} %bitcast.13, f32[4,128]{1,0:T(4,128)S(1)} %get-tuple-element.57.outer_ref, f32[4,128]{1,0:T(4,128)S(1)} %get-tuple-element.40.inner_ref, s32[1,1152]{1,0:T(1,128)S(1)} %get-tuple-element.58.cell_ref, ...), custom_call_target="tpu_custom_call" | custom-call | tf_op jit(solution)/shard_map/edges/pallas_call | solution.py:699
  43.6 13.1 %all_to_all.28 = f32[64,1,128]{2,1,0:T(1,128)S(1)} all-to-all(f32[64,1,128]{2,1,0:T(1,128)S(1)} %bitcast.14), channel_id=1, replica_groups=mesh['gx'=8,'gy'=8,'gz'=8] {'gx','gy'}, dimensions={0} | all-to-all | bytes 65536 | tf_op jit(solution)/shard_map/all_to_all | solution.py:721
  56.7 0.3 columns_back.1
  56.9 9.0 %all_to_all.29.recv_ref = f32[8,4,128]{2,1,0:T(4,128)S(1)} all-to-all(f32[8,4,128]{2,1,0:T(4,128)S(1)} %get-tuple-element.70), channel_id=1, replica_groups=mesh['gx'=8,'gy'=8,'gz'=8] {'gz'}, dimensions={0} | all-to-all | bytes 32768 | tf_op jit(solution)/shard_map/all_to_all | solution.py:728
  65.9 0.8 %forces.1 = (f32[3,1,72]{2,1,0:T(1,128)}, f32[1,72]{1,0:T(1,128)}, f32[3,3]{1,0:T(4,128)}) custom-call(f32[8,4,128]{2,1,0:T(4,128)S(1)} %all_to_all.29.recv_ref, f32[8,128]{1,0:T(8,128)S(1)} %get-tuple-element.71.keep_ref, f32[8,72]{1,0:T(8,128)S(1)} %get-tuple-element.72.local_ref, bf16[72,128]{1,0:T(8,128)(2,1)S(1)} %get-tuple-element.73.hot_ref), custom_call_target="tpu_custom_call" | custom-call | tf_op jit(solution)/shard_map/forces/pallas_call | solution.py:729
Async XLA Ops:
  2.0 14.7 %collective-permute-start = (f32[2,128]{1,0:T(2,128)S(1)}, f32[2,128]{1,0:T(2,128)S(1)}, u32[]{:S(2)}, u32[]{:S(2)}) collective-permute-start(f32[2,128]{1,0:T(2,128)S(1)} %get-tuple-element.41), channel_id=1, source_target_pairs={{0,7},{1,2},{2,1},{3,4},{4,3},{5,6},{6,5},{7,0},{8,15},{9,10},{10,... | collective-permute-start | bytes 3080 | tf_op jit(solution)/shard_map/ppermute | solution.py:665
  13.5 4.3 %collective-permute-start.1 = (f32[2,128]{1,0:T(2,128)S(1)}, f32[2,128]{1,0:T(2,128)S(1)}, u32[]{:S(2)}, u32[]{:S(2)}) collective-permute-start(f32[2,128]{1,0:T(2,128)S(1)} %get-tuple-element.42), channel_id=1, source_target_pairs={{0,1},{1,0},{2,3},{3,2},{4,5},{5,4},{6,7},{7,6},{8,9},{9,8},{10,11... | collective-permute-start | bytes 3080 | tf_op jit(solution)/shard_map/ppermute | solution.py:666

commit v4 on v3

--- a/solution.py
+++ b/solution.py
@@ -30,14 +30,12 @@
 
 
 def tables():
-    routes = np.zeros((512, 256), np.float32)
+    routes = np.zeros((256, 256), np.float32)
     layers = {0: 0, 3: 64, 1: LANES, 2: LANES + 64}
     for k in range(4):
         for n, (dx, dy) in enumerate(STEPS):
             for m, (x, y) in face(dx, dy):
-                place, column = n * 32 + k * 8 + m, layers[k] + x * 6 + y
-                routes[column, place] = 1.0
-                routes[256 + place, column] = 1.0
+                routes[layers[k] + x * 6 + y, n * 32 + k * 8 + m] = 1.0
     return routes
 
 
@@ -100,6 +98,10 @@
     return jnp.where(at < 36, 2 * at + (lane >> 6), -1)
 
 
+def pick_lanes(x, lanes):
+    return jnp.take_along_axis(x, lanes, axis=1, mode="promise_in_bounds")
+
+
 def low_half(x, y):
     return jnp.where(iota(x.shape, 1) < 64, x, y)
 
@@ -109,16 +111,17 @@
 
 
 def send_kernel(*refs):
-    sources, (both_ref, first_ref, second_ref, hot_ref), copied = refs[:13], refs[13:17], refs[17:29]
-    pos_ref, kind_ref, site_ref = copied[0], copied[1], refs[29]
-    copies = start_fetch(sources, (site_ref,) + copied, refs[30])
+    sources, (both_ref, first_ref, second_ref, hot_ref), copied = refs[:10], refs[10:14], refs[14:23]
+    pos_ref, kind_ref, site_ref = copied[0], copied[1], refs[23]
+    copies = start_fetch(sources, (site_ref,) + copied, refs[24])
     for copy in copies[:3]:
         copy.wait()
     rows = atom_rows(pos_ref, kind_ref)
-    hot = as_hot(iota((ATOMS, ATOMS), 0) == site_ref[...])
-    pick = as_hot(iota((ATOMS, LANES), 0) == lane_sites()[0:1])
-    placed = jnp.dot(hot, pick, preferred_element_type=F32).astype(BF16)
-    both = exact_dot(rows, placed)
+    sites = lane_sites()
+    wide = jnp.concatenate([site_ref[...], jnp.zeros((1, LANES - ATOMS), jnp.int32)], axis=1)
+    atoms = pick_lanes(jnp.broadcast_to(wide, (8, LANES)), jnp.maximum(sites, 0))
+    both = pick_lanes(jnp.concatenate([rows, jnp.zeros((8, LANES - ATOMS), F32)], axis=1), atoms)
+    both = jnp.where(sites >= 0, both, 0.0)
     turned = pltpu.roll(both, 64, 1)
     down = [low_half(both[c : c + 1], turned[c + 1 : c + 2]) for c in (0, 2)]
     up = [low_half(turned[c : c + 1], both[c + 1 : c + 2]) for c in (0, 2)]
@@ -126,7 +129,7 @@
         first_ref[c : c + 1] = jnp.where(even_layer(), down[c], up[c])
         second_ref[c : c + 1] = jnp.where(even_layer(), up[c], down[c])
     both_ref[...] = both[:4]
-    hot_ref[...] = placed
+    hot_ref[...] = as_hot(iota((ATOMS, LANES), 0) == jnp.where(sites >= 0, atoms, -1)[0:1])
     for copy in copies[3:]:
         copy.wait()
 
@@ -171,7 +174,7 @@
     return lax.rem(gx + (dx + COUNT), COUNT) * COUNT + lax.rem(gy + (dy + COUNT), COUNT)
 
 
-def column_kernel(inner_ref, first_ref, second_ref, routes_ref, tie_ref, msg_ref, outer_ref):
+def column_kernel(inner_ref, first_ref, second_ref, routes_ref, msg_ref, outer_ref):
     first, second = first_ref[...], second_ref[...]
     below = jnp.where(even_layer(), first, second)
     above = jnp.where(even_layer(), second, first)
@@ -183,7 +186,7 @@
     outer = pad_rows(jnp.concatenate(rows, axis=0))
     outer_ref[...] = outer[:4]
     column = jnp.concatenate([outer, pad_rows(inner_ref[...])], axis=1)
-    rows = to_rows(exact_dot(column, routes_ref[:256]))
+    rows = to_rows(exact_dot(column, routes_ref[...]))
     msg_ref[...] = jnp.zeros_like(msg_ref)
     for n in range(8):
         msg_ref[pl.ds(neighbour(n), 1), :] = rows[n]
@@ -221,9 +224,13 @@
 
 
 def prepare_kernel(count_ref, *refs):
-    inputs, outputs = refs[:11], refs[11:]
+    inputs, sources, outputs, buffers, sems = refs[:9], refs[9:12], refs[12:24], refs[24:26], refs[26]
+    copies = start_fetch(sources, buffers + outputs[11:], sems)
     make_slots(count_ref, inputs[:4], outputs[:4])
-    make_weights(inputs[4:], outputs[4:])
+    for copy in copies[:2]:
+        copy.wait()
+    make_weights(inputs[4:] + buffers, outputs[4:11])
+    copies[2].wait()
 
 
 def make_slots(count_ref, buffers, outputs):
@@ -278,7 +285,7 @@
 
 def make_weights(buffers, outputs):
     win_ref, w3_ref, wlat_ref, wlat_t_ref, w3_t_ref, win_t_ref, read_ref = outputs
-    w_in_ref, w_two_ref, w_env_ref, w_value_ref, w_latent_ref, w_out_ref, readout_ref = buffers
+    w_out_ref, readout_ref, w_two_ref, w_env_ref, w_value_ref, w_latent_ref, w_in_ref = buffers
     w_in_t = w_in_ref[...]
     win_ref[...] = cat_of(w_in_t.T)
     w_two = w_two_ref[...]
@@ -581,7 +588,7 @@
 
 def middle_kernel(recv_ref, ext_ref, routes_ref, msg_ref, keep_ref):
     columns = from_rows([recv_ref[pl.ds(neighbour(n), 1), :] for n in range(8)])
-    sums = exact_dot(jnp.concatenate(columns, axis=1), routes_ref[256:], 2) + pad_rows(ext_ref[...])
+    sums = exact_dot_nt(jnp.concatenate(columns, axis=1), routes_ref[...], 2) + pad_rows(ext_ref[...])
     total = jnp.sum(recv_ref[...], axis=0, keepdims=True)
     message = jnp.concatenate([sums[:3, :LANES], total], axis=0)
     msg_ref[...] = jnp.broadcast_to(message[None], (COUNT, 4, LANES))
@@ -644,16 +651,14 @@
         species,
         edge_center,
         edge_other,
-        w_in.T,
+        w_out,
+        readout.reshape(1, 64),
         w_two,
         w_env,
         w_value,
-        w_latent,
-        w_out,
-        readout.reshape(1, 64),
-        jnp.asarray(ROUTES, BF16),
-    )
-    own, first, second, hot, *copied, routes = pl.pallas_call(
+    )
+    weights = (w_latent, w_in.T, jnp.asarray(ROUTES, BF16))
+    own, first, second, hot, *copied = pl.pallas_call(
         send_kernel,
         in_specs=[hbm] * len(inputs),
         out_shape=(shape(*half), shape(2, LANES), shape(2, LANES), shape(ATOMS, LANES, dtype=BF16))
@@ -666,9 +671,9 @@
     second = lax.ppermute(second, "gz", [(i, i ^ 1) for i in range(COUNT)])
 
     vmem = pl.BlockSpec(memory_space=pltpu.VMEM)
-    prepared = pl.pallas_call(
+    *prepared, routes = pl.pallas_call(
         prepare_kernel,
-        in_specs=[pl.BlockSpec(memory_space=pltpu.SMEM)] + [vmem] * 11,
+        in_specs=[pl.BlockSpec(memory_space=pltpu.SMEM)] + [vmem] * len(copied) + [hbm] * len(weights),
         out_shape=(
             shape(1, EDGES, dtype=jnp.int32),
             shape(1, EDGES),
@@ -681,11 +686,14 @@
             shape(256, 384, dtype=BF16),
             shape(32, 256, dtype=BF16),
             shape(128, LANES),
+            shape(256, 256, dtype=BF16),
         ),
+        scratch_shapes=[pltpu.VMEM(x.shape, x.dtype) for x in weights[:-1]]
+        + [pltpu.SemaphoreType.DMA((len(weights),))],
         compiler_params=params(),
         cost_estimate=pl.CostEstimate(flops=10_000_000, bytes_accessed=2_000_000, transcendentals=0),
         name="slots_and_weights",
-    )(edge_count, *copied)
+    )(edge_count, *copied, *in_hbm(*weights))
 
     planes = (COUNT * COUNT, LANES)
     column, outer = pl.pallas_call(
@@ -693,7 +701,7 @@
         out_shape=(shape(*planes), shape(*half)),
         compiler_params=params(),
         name="column",
-    )(own, first, second, routes, prepared[3])
+    )(own, first, second, routes)
     arrived = lax.all_to_all(column, ("gx", "gy"), 0, 0)
 
     message, extended_grad, local_grad = pl.pallas_call(

time: 67 us -> 67 us (level)
  waiting for transfers between devices: 1.09 us -> 0.01 us
  Pallas kernels: 7.6 us -> 8.39 us
    pallas_call x1, Pallas kernels: 0.63 us -> 1.73 us  [body(): pl.pallas_call(prepare_kernel, in_specs=[pl.BlockSpec(memory_space=pltpu....]
    ppermute x1, waiting for transfers between devices: 1.09 us -> 0.01 us  [body(): second = lax.ppermute(second, 'gz', [(i, i ^ 1) for i in range(COUNT)])]
  transfers between devices with their start and end apart: 2 -> 2, of which waited for: 1 -> 0; matrix products, arithmetic and copies ran while one was open for 0% -> 0% of each run, Pallas kernels for 1% -> 3%
where the time goes in v4:
time: 67 us; the launch traced here: 66.6 us
  blocking collectives  43.5 us (65%)
  starting transfers between devices  13.4 us (20%)
  Pallas kernels  8.39 us (13%)
  between operations  1.35 us (2%)
    all_to_all x1, blocking collectives, body(): arrived = lax.all_to_all(column, ('gx', 'gy'), 0, 0)  21.2 us
    all_to_all x1, blocking collectives, body(): returned = lax.all_to_all(message, ('gx', 'gy'), 0, 0)  13.1 us
    ppermute x1, starting transfers between devices, body(): lax.ppermute(first, 'gz', [(i, (i - 1 ^ 1) + 1 & 7) for i in range(COUNT)])  11.5 us
    all_to_all x1, blocking collectives, body(): closing = lax.all_to_all(layers, 'gz', 0, 0)  9.2 us
    pallas_call x1, Pallas kernels, body(): pl.pallas_call(main_kernel, out_shape=(shape(*planes), shape(4, 256), sha...  4.25 us
    ppermute x1, starting transfers between devices, body(): second = lax.ppermute(second, 'gz', [(i, i ^ 1) for i in range(COUNT)])  1.92 us
    pallas_call x1, Pallas kernels, body(): pl.pallas_call(prepare_kernel, in_specs=[pl.BlockSpec(memory_space=pltpu....  1.73 us
  transfers between devices with their start and end apart: 2, of which 0 were waited for; matrix products, arithmetic and copies ran while one was open for 0% of the time, Pallas kernels for 3%

profile of v4, /device:TPU:1, one launch (start us, length us, event | category | flops | bytes accessed | tf_op | source)
XLA Modules:
  0.0 66.6 jit_solution(3902473345642174071)
XLA Ops:
  0.6 1.0 %sites.1 = (f32[4,128]{1,0:T(4,128)S(1)}, f32[2,128]{1,0:T(2,128)S(1)}, f32[2,128]{1,0:T(2,128)S(1)}, bf16[72,128]{1,0:T(8,128)(2,1)S(1)}, f32[3,1,72]{2,1,0:T(1...) custom-call(s32[1,72]{1,0:T(1,128)} %refs_0_.1, ...), custom_call_target="tpu_custom_call" | custom-call | tf_op jit(solution)/shard_map/sites/pallas_call | solution.py:661
  1.7 11.5 %collective-permute-start = (f32[2,128]{1,0:T(2,128)S(1)}, f32[2,128]{1,0:T(2,128)S(1)}, u32[]{:S(2)}, u32[]{:S(2)}) collective-permute-start(f32[2,128]{1,0:T(2,128)S(1)} %get-tuple-element.39), channel_id=1, source_target_pairs={{0,7},{1,2},{2,1},{3,4},{4,3},{5,6},{6,5},{7,0},{8,15},{9,10},{10,... | collective-permute-start | bytes 3080 | tf_op jit(solution)/shard_map/ppermute | solution.py:670
  13.2 1.9 %collective-permute-start.1 = (f32[2,128]{1,0:T(2,128)S(1)}, f32[2,128]{1,0:T(2,128)S(1)}, u32[]{:S(2)}, u32[]{:S(2)}) collective-permute-start(f32[2,128]{1,0:T(2,128)S(1)} %get-tuple-element.40), channel_id=1, source_target_pairs={{0,1},{1,0},{2,3},{3,2},{4,5},{5,4},{6,7},{7,6},{8,9},{9,8},{10,11... | collective-permute-start | bytes 3080 | tf_op jit(solution)/shard_map/ppermute | solution.py:671
  15.7 1.7 %slots_and_weights.1 = (s32[1,1152]{1,0:T(1,128)S(1)}, f32[1,1152]{1,0:T(1,128)S(1)}, f32[8,256]{1,0:T(8,128)S(1)}, f32[8,512]{1,0:T(8,128)S(1)}, bf16[256,32]{1...) custom-call(s32[1]{0:T(128)S(6)} %copy.19.count_ref, ...), custom_call_target="tpu_custom_call" | custom-call | flops 10000000 | bytes 2000000 | tf_op jit(solution)/shard_map/slots_and_weights/pallas_call | solution.py:674
  17.5 0.0 collective-permute-done.first_ref
  17.5 0.0 collective-permute-done.1.second_ref
  17.5 0.4 column.1
  17.9 21.2 %all_to_all.27 = f32[64,1,128]{2,1,0:T(1,128)S(1)} all-to-all(f32[64,1,128]{2,1,0:T(1,128)S(1)} %bitcast.15), channel_id=1, replica_groups=mesh['gx'=8,'gy'=8,'gz'=8] {'gx','gy'}, dimensions={0} | all-to-all | bytes 65536 | tf_op jit(solution)/shard_map/all_to_all | solution.py:705
  39.0 4.2 %edges.1 = (f32[64,128]{1,0:T(8,128)S(1)}, f32[4,256]{1,0:T(4,128)S(1)}, f32[8,72]{1,0:T(8,128)S(1)}) custom-call(f32[64,128]{1,0:T(8,128)S(1)} %bitcast.13, f32[4,128]{1,0:T(4,128)S(1)} %get-tuple-element.52.outer_ref, f32[4,128]{1,0:T(4,128)S(1)} %get-tuple-element.38.inner_ref, s32[1,1152]{1,0:T(1,128)S(1)} %get-tuple-element.53.cell_ref, ...), custom_call_target="tpu_custom_call" | custom-call | tf_op jit(solution)/shard_map/edges/pallas_call | solution.py:707
  43.3 13.1 %all_to_all.28 = f32[64,1,128]{2,1,0:T(1,128)S(1)} all-to-all(f32[64,1,128]{2,1,0:T(1,128)S(1)} %bitcast.14), channel_id=1, replica_groups=mesh['gx'=8,'gy'=8,'gz'=8] {'gx','gy'}, dimensions={0} | all-to-all | bytes 65536 | tf_op jit(solution)/shard_map/all_to_all | solution.py:729
  56.4 0.3 columns_back.1
  56.6 9.2 %all_to_all.29.recv_ref = f32[8,4,128]{2,1,0:T(4,128)S(1)} all-to-all(f32[8,4,128]{2,1,0:T(4,128)S(1)} %get-tuple-element.66), channel_id=1, replica_groups=mesh['gx'=8,'gy'=8,'gz'=8] {'gz'}, dimensions={0} | all-to-all | bytes 32768 | tf_op jit(solution)/shard_map/all_to_all | solution.py:736
  65.8 0.8 %forces.1 = (f32[3,1,72]{2,1,0:T(1,128)}, f32[1,72]{1,0:T(1,128)}, f32[3,3]{1,0:T(4,128)}) custom-call(f32[8,4,128]{2,1,0:T(4,128)S(1)} %all_to_all.29.recv_ref, f32[8,128]{1,0:T(8,128)S(1)} %get-tuple-element.67.keep_ref, f32[8,72]{1,0:T(8,128)S(1)} %get-tuple-element.68.local_ref, bf16[72,128]{1,0:T(8,128)(2,1)S(1)} %get-tuple-element.69.hot_ref), custom_call_target="tpu_custom_call" | custom-call | tf_op jit(solution)/shard_map/forces/pallas_call | solution.py:737
Async XLA Ops:
  1.7 15.8 %collective-permute-start = (f32[2,128]{1,0:T(2,128)S(1)}, f32[2,128]{1,0:T(2,128)S(1)}, u32[]{:S(2)}, u32[]{:S(2)}) collective-permute-start(f32[2,128]{1,0:T(2,128)S(1)} %get-tuple-element.39), channel_id=1, source_target_pairs={{0,7},{1,2},{2,1},{3,4},{4,3},{5,6},{6,5},{7,0},{8,15},{9,10},{10,... | collective-permute-start | bytes 3080 | tf_op jit(solution)/shard_map/ppermute | solution.py:670
  13.2 4.3 %collective-permute-start.1 = (f32[2,128]{1,0:T(2,128)S(1)}, f32[2,128]{1,0:T(2,128)S(1)}, u32[]{:S(2)}, u32[]{:S(2)}) collective-permute-start(f32[2,128]{1,0:T(2,128)S(1)} %get-tuple-element.40), channel_id=1, source_target_pairs={{0,1},{1,0},{2,3},{3,2},{4,5},{5,4},{6,7},{7,6},{8,9},{9,8},{10,11... | collective-permute-start | bytes 3080 | tf_op jit(solution)/shard_map/ppermute | solution.py:671

commit v5 on v4

--- a/solution.py
+++ b/solution.py
@@ -111,9 +111,9 @@
 
 
 def send_kernel(*refs):
-    sources, (both_ref, first_ref, second_ref, hot_ref), copied = refs[:10], refs[10:14], refs[14:23]
-    pos_ref, kind_ref, site_ref = copied[0], copied[1], refs[23]
-    copies = start_fetch(sources, (site_ref,) + copied, refs[24])
+    sources, (both_ref, first_ref, second_ref, hot_ref), copied = refs[:12], refs[12:16], refs[16:27]
+    pos_ref, kind_ref, site_ref = copied[0], copied[1], refs[27]
+    copies = start_fetch(sources, (site_ref,) + copied, refs[28])
     for copy in copies[:3]:
         copy.wait()
     rows = atom_rows(pos_ref, kind_ref)
@@ -224,13 +224,12 @@
 
 
 def prepare_kernel(count_ref, *refs):
-    inputs, sources, outputs, buffers, sems = refs[:9], refs[9:12], refs[12:24], refs[24:26], refs[26]
-    copies = start_fetch(sources, buffers + outputs[11:], sems)
+    inputs, table, outputs, sem = refs[:11], refs[11], refs[12:24], refs[24]
+    copy = pltpu.make_async_copy(table, outputs[11], sem)
+    copy.start()
     make_slots(count_ref, inputs[:4], outputs[:4])
-    for copy in copies[:2]:
-        copy.wait()
-    make_weights(inputs[4:] + buffers, outputs[4:11])
-    copies[2].wait()
+    make_weights(inputs[4:], outputs[4:11])
+    copy.wait()
 
 
 def make_slots(count_ref, buffers, outputs):
@@ -656,8 +655,9 @@
         w_two,
         w_env,
         w_value,
-    )
-    weights = (w_latent, w_in.T, jnp.asarray(ROUTES, BF16))
+        w_latent,
+        w_in.T,
+    )
     own, first, second, hot, *copied = pl.pallas_call(
         send_kernel,
         in_specs=[hbm] * len(inputs),
@@ -673,7 +673,7 @@
     vmem = pl.BlockSpec(memory_space=pltpu.VMEM)
     *prepared, routes = pl.pallas_call(
         prepare_kernel,
-        in_specs=[pl.BlockSpec(memory_space=pltpu.SMEM)] + [vmem] * len(copied) + [hbm] * len(weights),
+        in_specs=[pl.BlockSpec(memory_space=pltpu.SMEM)] + [vmem] * len(copied) + [hbm],
         out_shape=(
             shape(1, EDGES, dtype=jnp.int32),
             shape(1, EDGES),
@@ -688,12 +688,11 @@
             shape(128, LANES),
             shape(256, 256, dtype=BF16),
         ),
-        scratch_shapes=[pltpu.VMEM(x.shape, x.dtype) for x in weights[:-1]]
-        + [pltpu.SemaphoreType.DMA((len(weights),))],
+        scratch_shapes=[pltpu.SemaphoreType.DMA(())],
         compiler_params=params(),
         cost_estimate=pl.CostEstimate(flops=10_000_000, bytes_accessed=2_000_000, transcendentals=0),
         name="slots_and_weights",
-    )(edge_count, *copied, *in_hbm(*weights))
+    )(edge_count, *copied, *in_hbm(jnp.asarray(ROUTES, BF16)))
 
     planes = (COUNT * COUNT, LANES)
     column, outer = pl.pallas_call(

time: 67 us -> 66.9 us (level)
  transfers between devices with their start and end apart: 2 -> 2, of which waited for: 0 -> 1; matrix products, arithmetic and copies ran while one was open for 0% -> 0% of each run, Pallas kernels for 3% -> 2%
where the time goes in v5:
time: 66.9 us; the launch traced here: 66.6 us
  blocking collectives  43.3 us (65%)
  starting transfers between devices  13.4 us (20%)
  Pallas kernels  7.89 us (12%)
  between operations  1.34 us (2%)
    all_to_all x1, blocking collectives, body(): arrived = lax.all_to_all(column, ('gx', 'gy'), 0, 0)  21.2 us
    all_to_all x1, blocking collectives, body(): returned = lax.all_to_all(message, ('gx', 'gy'), 0, 0)  13.1 us
    ppermute x1, starting transfers between devices, body(): lax.ppermute(first, 'gz', [(i, (i - 1 ^ 1) + 1 & 7) for i in range(COUNT)])  11.5 us
    all_to_all x1, blocking collectives, body(): closing = lax.all_to_all(layers, 'gz', 0, 0)  9 us
    pallas_call x1, Pallas kernels, body(): pl.pallas_call(main_kernel, out_shape=(shape(*planes), shape(4, 256), sha...  4.25 us
    ppermute x1, starting transfers between devices, body(): second = lax.ppermute(second, 'gz', [(i, i ^ 1) for i in range(COUNT)])  1.92 us
  transfers between devices with their start and end apart: 2, of which 1 were waited for; matrix products, arithmetic and copies ran while one was open for 0% of the time, Pallas kernels for 2%

profile of v5, /device:TPU:1, one launch (start us, length us, event | category | flops | bytes accessed | tf_op | source)
XLA Modules:
  0.0 66.6 jit_solution(16908421072654857660)
XLA Ops:
  0.6 1.2 %sites.1 = (f32[4,128]{1,0:T(4,128)S(1)}, f32[2,128]{1,0:T(2,128)S(1)}, f32[2,128]{1,0:T(2,128)S(1)}, bf16[72,128]{1,0:T(8,128)(2,1)S(1)}, f32[3,1,72]{2,1,0:T(1...) custom-call(s32[1,72]{1,0:T(1,128)} %refs_0_.1, ...), custom_call_target="tpu_custom_call" | custom-call | tf_op jit(solution)/shard_map/sites/pallas_call | solution.py:661
  1.8 11.5 %collective-permute-start = (f32[2,128]{1,0:T(2,128)S(1)}, f32[2,128]{1,0:T(2,128)S(1)}, u32[]{:S(2)}, u32[]{:S(2)}) collective-permute-start(f32[2,128]{1,0:T(2,128)S(1)} %get-tuple-element.41), channel_id=1, source_target_pairs={{0,7},{1,2},{2,1},{3,4},{4,3},{5,6},{6,5},{7,0},{8,15},{9,10},{10,... | collective-permute-start | bytes 3080 | tf_op jit(solution)/shard_map/ppermute | solution.py:670
  13.3 1.9 %collective-permute-start.1 = (f32[2,128]{1,0:T(2,128)S(1)}, f32[2,128]{1,0:T(2,128)S(1)}, u32[]{:S(2)}, u32[]{:S(2)}) collective-permute-start(f32[2,128]{1,0:T(2,128)S(1)} %get-tuple-element.42), channel_id=1, source_target_pairs={{0,1},{1,0},{2,3},{3,2},{4,5},{5,4},{6,7},{7,6},{8,9},{9,8},{10,11... | collective-permute-start | bytes 3080 | tf_op jit(solution)/shard_map/ppermute | solution.py:671
  15.9 1.1 %slots_and_weights.1 = (s32[1,1152]{1,0:T(1,128)S(1)}, f32[1,1152]{1,0:T(1,128)S(1)}, f32[8,256]{1,0:T(8,128)S(1)}, f32[8,512]{1,0:T(8,128)S(1)}, bf16[256,32]{1...) custom-call(s32[1]{0:T(128)S(6)} %copy.19.count_ref, ...), custom_call_target="tpu_custom_call" | custom-call | flops 10000000 | bytes 2000000 | tf_op jit(solution)/shard_map/slots_and_weights/pallas_call | solution.py:674
  17.0 0.0 collective-permute-done.first_ref
  17.0 0.7 collective-permute-done.1.second_ref
  17.6 0.4 column.1
  18.0 21.2 %all_to_all.27 = f32[64,1,128]{2,1,0:T(1,128)S(1)} all-to-all(f32[64,1,128]{2,1,0:T(1,128)S(1)} %bitcast.15), channel_id=1, replica_groups=mesh['gx'=8,'gy'=8,'gz'=8] {'gx','gy'}, dimensions={0} | all-to-all | bytes 65536 | tf_op jit(solution)/shard_map/all_to_all | solution.py:704
  39.2 4.3 %edges.1 = (f32[64,128]{1,0:T(8,128)S(1)}, f32[4,256]{1,0:T(4,128)S(1)}, f32[8,72]{1,0:T(8,128)S(1)}) custom-call(f32[64,128]{1,0:T(8,128)S(1)} %bitcast.13, f32[4,128]{1,0:T(4,128)S(1)} %get-tuple-element.56.outer_ref, f32[4,128]{1,0:T(4,128)S(1)} %get-tuple-element.40.inner_ref, s32[1,1152]{1,0:T(1,128)S(1)} %get-tuple-element.57.cell_ref, ...), custom_call_target="tpu_custom_call" | custom-call | tf_op jit(solution)/shard_map/edges/pallas_call | solution.py:706
  43.5 13.1 %all_to_all.28 = f32[64,1,128]{2,1,0:T(1,128)S(1)} all-to-all(f32[64,1,128]{2,1,0:T(1,128)S(1)} %bitcast.14), channel_id=1, replica_groups=mesh['gx'=8,'gy'=8,'gz'=8] {'gx','gy'}, dimensions={0} | all-to-all | bytes 65536 | tf_op jit(solution)/shard_map/all_to_all | solution.py:728
  56.5 0.3 columns_back.1
  56.8 9.0 %all_to_all.29.recv_ref = f32[8,4,128]{2,1,0:T(4,128)S(1)} all-to-all(f32[8,4,128]{2,1,0:T(4,128)S(1)} %get-tuple-element.70), channel_id=1, replica_groups=mesh['gx'=8,'gy'=8,'gz'=8] {'gz'}, dimensions={0} | all-to-all | bytes 32768 | tf_op jit(solution)/shard_map/all_to_all | solution.py:735
  65.8 0.8 %forces.1 = (f32[3,1,72]{2,1,0:T(1,128)}, f32[1,72]{1,0:T(1,128)}, f32[3,3]{1,0:T(4,128)}) custom-call(f32[8,4,128]{2,1,0:T(4,128)S(1)} %all_to_all.29.recv_ref, f32[8,128]{1,0:T(8,128)S(1)} %get-tuple-element.71.keep_ref, f32[8,72]{1,0:T(8,128)S(1)} %get-tuple-element.72.local_ref, bf16[72,128]{1,0:T(8,128)(2,1)S(1)} %get-tuple-element.73.hot_ref), custom_call_target="tpu_custom_call" | custom-call | tf_op jit(solution)/shard_map/forces/pallas_call | solution.py:736
Async XLA Ops:
  1.8 15.2 %collective-permute-start = (f32[2,128]{1,0:T(2,128)S(1)}, f32[2,128]{1,0:T(2,128)S(1)}, u32[]{:S(2)}, u32[]{:S(2)}) collective-permute-start(f32[2,128]{1,0:T(2,128)S(1)} %get-tuple-element.41), channel_id=1, source_target_pairs={{0,7},{1,2},{2,1},{3,4},{4,3},{5,6},{6,5},{7,0},{8,15},{9,10},{10,... | collective-permute-start | bytes 3080 | tf_op jit(solution)/shard_map/ppermute | solution.py:670
  13.3 4.3 %collective-permute-start.1 = (f32[2,128]{1,0:T(2,128)S(1)}, f32[2,128]{1,0:T(2,128)S(1)}, u32[]{:S(2)}, u32[]{:S(2)}) collective-permute-start(f32[2,128]{1,0:T(2,128)S(1)} %get-tuple-element.42), channel_id=1, source_target_pairs={{0,1},{1,0},{2,3},{3,2},{4,5},{5,4},{6,7},{7,6},{8,9},{9,8},{10,11... | collective-permute-start | bytes 3080 | tf_op jit(solution)/shard_map/ppermute | solution.py:671
